TPU v7x, 32 devices: a whole 2x2x4 slice. The times are simulated.
32 devices in a mesh: dp: 4 (over x, core), space: 8 (over z, y).
Axes of the slice: x: 2, y: 2, z: 4, core: 2. Of those that a mesh axis runs over, the one named last changes fastest.
Arguments:
- volume: bfloat16 [4, 4, 64, 8, 256], P('dp', None, 'space'), may hold values from -6 to 6
- first_filters: bfloat16 [16, 4, 3, 3, 3], replicated, may hold values from -0.625 to 0.625
- first_biases: float32 [16], replicated, may hold values from -0.5 to 0.5
- second_filters: bfloat16 [32, 16, 3, 3, 3], replicated, may hold values from -0.3125 to 0.3125
- second_biases: float32 [32], replicated, may hold values from -0.5 to 0.5
- cotangent: bfloat16 [4, 32, 32, 4, 128], P('dp', None, 'space'), may hold values from -12 to 12
Outputs:
- activations: bfloat16 [4, 32, 32, 4, 128], P('dp', None, 'space')
- pooled_grad: bfloat16 [4, 16, 32, 4, 128], P('dp', None, 'space')
- gradient_one: float32 [16, 4, 3, 3, 3], replicated
- shift_one: float32 [16], replicated
- gradient_two: float32 [32, 16, 3, 3, 3], replicated
- shift_two: float32 [32], replicated
All inputs are finite; a program needn't handle non-finite values.
Results may differ from a plain program's by a relative error of at most 0.015.
The roundings to bfloat16 on the way count: a program that leaves them out, or rounds other values in their place, can miss the bound.
Values may be sent and summed in bfloat16 or wider, within the bound.
A program may use at most 128 MiB of HBM per device.

v0:
```python
import math

import jax
import jax.numpy as jnp
from jax import lax
from jax.sharding import PartitionSpec as P


def with_halo(block, sides, width):
    for axis, dim in sides:
        count = lax.axis_size(axis)
        forward = [(i, i + 1) for i in range(count - 1)]
        backward = [(target, source) for source, target in forward]
        low = lax.ppermute(
            lax.slice_in_dim(block, block.shape[dim] - width, None, axis=dim), axis, forward
        )
        high = lax.ppermute(lax.slice_in_dim(block, 0, width, axis=dim), axis, backward)
        block = jnp.concatenate([low, block, high], axis=dim)
    return block


def convolve(padded, kernel):
    return lax.conv_general_dilated(
        padded[None],
        kernel,
        (1, 1, 1),
        "VALID",
        dimension_numbers=("NCDHW", "OIDHW", "NCDHW"),
        preferred_element_type=jnp.float32,
    )[0]


def kernel_grad(padded, errors):
    result = lax.conv_general_dilated(
        padded[:, None],
        errors[:, None],
        (1, 1, 1),
        "VALID",
        dimension_numbers=("NCDHW", "OIDHW", "NCDHW"),
        preferred_element_type=jnp.float32,
    )
    return result.transpose(1, 0, 2, 3, 4)


def pad_plane(values):
    return jnp.pad(values, ((0, 0), (0, 0), (1, 1), (1, 1)))


def leaky_rectify(values):
    return jnp.where(values > 0, values, 0.3 * values)


def rectify_slope(values):
    return jnp.where(values > 0, 1.0, 0.3)


def mean_pool(values):
    extent = values.shape
    blocks = values.reshape(extent[0], extent[1] // 2, 2, extent[2] // 2, 2, extent[3] // 2, 2)
    return jnp.sum(blocks, axis=(2, 4, 6)) * 0.125


def spread_up(values):
    extent = values.shape
    grown = jnp.broadcast_to(
        values[:, :, None, :, None, :, None], (extent[0], extent[1], 2, extent[2], 2, extent[3], 2)
    )
    return grown.reshape(extent[0], 2 * extent[1], 2 * extent[2], 2 * extent[3])


def shards(volume, first_filters, first_biases, second_filters, second_biases, cotangent):
    sample = volume[0]
    target = cotangent[0]
    planes = sample.shape[1]
    rim_depth = 1
    haloed = with_halo(sample, (("space", 1),), 1)
    first_in = pad_plane(haloed)
    linear_one = convolve(first_in, first_filters) + first_biases[:, None, None, None]
    pooled = mean_pool(leaky_rectify(linear_one)).astype(jnp.bfloat16)
    pooled_ext = with_halo(pooled, (("space", 1),), rim_depth)
    second_in = pad_plane(pooled_ext)
    linear_wide = convolve(second_in, second_filters) + second_biases[:, None, None, None]
    delta_two = (target.astype(jnp.float32) * rectify_slope(linear_wide)).astype(jnp.bfloat16)
    delta_ext = with_halo(delta_two, (("space", 1),), 1)
    activations = leaky_rectify(linear_wide).astype(jnp.bfloat16)
    second_terms = (
        kernel_grad(second_in, delta_two),
        jnp.sum(delta_two.astype(jnp.float32), axis=(1, 2, 3)),
    )
    second_terms = lax.psum((second_terms[0], second_terms[1]), ("dp", "space"))
    flipped = jnp.flip(second_filters, (2, 3, 4)).transpose(1, 0, 2, 3, 4)
    pooled_grad = convolve(pad_plane(delta_ext), flipped).astype(jnp.bfloat16)
    stored_grad = lax.optimization_barrier(pooled_grad)
    delta_one = (
        spread_up(stored_grad.astype(jnp.float32)) * 0.125 * rectify_slope(linear_one)
    ).astype(jnp.bfloat16)
    first_terms = (
        kernel_grad(first_in, delta_one),
        jnp.sum(delta_one.astype(jnp.float32), axis=(1, 2, 3)),
    )
    first_terms = lax.psum((first_terms[0], first_terms[1]), ("dp", "space"))
    totals = (first_terms[0], first_terms[1], second_terms[0], second_terms[1])
    count_one = (
        lax.axis_size("dp") * lax.axis_size("space") * planes * sample.shape[2] * sample.shape[3]
    )
    scale_one = 1.0 / math.sqrt(count_one)
    scale_two = 1.0 / math.sqrt(count_one / 8)
    return (
        activations[None],
        pooled_grad[None],
        totals[0] * scale_one,
        totals[1] * scale_one,
        totals[2] * scale_two,
        totals[3] * scale_two,
    )


def solution(mesh):
    placed = (
        P("dp", None, "space", None, None),
        P(),
        P(),
        P(),
        P(),
        P("dp", None, "space", None, None),
    )
    return jax.shard_map(
        shards,
        mesh=mesh,
        in_specs=placed,
        out_specs=(
            P("dp", None, "space", None, None),
            P("dp", None, "space", None, None),
            P(),
            P(),
            P(),
            P(),
        ),
        check_vma=False,
    )
```

profile of v0, /device:TPU:0, one launch (start us, length us, event | category | flops | bytes accessed | tf_op | source)
XLA Modules:
  0.0 450.4 jit_solution(8624925857480295657)
XLA Ops:
  0.6 0.8 fusion.76
  1.4 4.9 %collective-permute-start = (bf16[4,1,8,256]{3,2,1,0:T(8,128)(2,1)S(1)}, bf16[4,1,8,256]{3,2,1,0:T(8,128)(2,1)S(1)}, u32[]{:S(2)}, u32[]{:S(2)}) collective-permute-start(bf16[4,1,8,256]{3,2,1,0:T(8,128)(2,1)S(1)} %get-tuple-element.60), channel_id=1, source_target_pairs={{0,1},{1,2},{2,3},{3,4},{4,5},{5,6},{6,7},{8,9},{9,10},{10,11},{11... | collective-permute-start | bytes 49160 | tf_op jit(solution)/shard_map/ppermute | solution.py:14
  6.3 1.3 collective-permute-start.1
  7.6 1.3 copy.164
  9.0 3.0 collective-permute-done.1
  11.9 1.3 fusion.79
  13.3 0.8 reshape.137
  14.1 4.3 copy.155
  18.4 1.1 slice.34
  19.6 25.4 %fusion = (f32[8,8,8,33,16]{4,2,3,1,0:T(8,128)}, f32[8,8,8,33,16]{4,2,3,1,0:T(8,128)}) fusion(f32[16]{0:T(128)S(1)} %copy-done.12, bf16[16,4,3,3,3]{0,1,4,3,2:T(4,128)(2,1)S(1)} %copy-done.16, bf16[4,10,10,1,7,2]{4,0,5,2,1,3:T(4,128)(2,1)S(1)} %slice.34, bf16[4,10,10,1,8,33]{4,0,5,2,1,3:T(4,128)(2,1)} %copy.155, pred[8,33]{0,1:T(8,128)(4,1)S(1)} %copy-done.17), kind=kOutput, calls=%fused_computation.2 | convolution fusion | flops 60145920 | bytes 2388872 | tf_op jit(solution)/shard_map/conv_general_dilated | solution.py:23
  45.0 8.5 %copy.156 = f32[8,8,8,33,16]{3,2,4,1,0:T(8,128)} copy(f32[8,8,8,33,16]{4,2,3,1,0:T(8,128)} %get-tuple-element.65) | data formatting | bytes 2162688 | tf_op jit(solution)/shard_map/conv_general_dilated | solution.py:23
  53.5 3.5 reshape.99
  57.1 4.8 %copy.157 = f32[1,16,8,8,256]{1,4,3,2,0:T(8,128)} copy(f32[1,16,8,8,256]{4,1,3,2,0:T(8,128)S(1)} %slice_bitcast_fusion) | data formatting | bytes 2097152 | tf_op jit(solution)/shard_map/conv_general_dilated | solution.py:23
  62.0 12.8 %fusion.2 = f32[16,4,4,128]{0,3,2,1:T(8,128)S(1)} fusion(f32[16,4,2,4,2,128,2]{0,6,5,4,3,2,1:T(2,128)} %bitcast.110, f32[16]{0:T(128)S(1)} %copy-done.12), kind=kLoop, calls=%fused_computation.6 | loop fusion | flops 1277952 | bytes 1179712 | tf_op jit(solution)/shard_map/reduce_sum | solution.py:60
  75.6 5.0 %collective-permute-start.2 = (bf16[16,1,4,128]{0,3,2,1:T(8,128)(2,1)}, bf16[16,1,4,128]{0,3,2,1:T(8,128)(2,1)}, u32[]{:S(2)}, u32[]{:S(2)}) collective-permute-start(bf16[16,1,4,128]{0,3,2,1:T(8,128)(2,1)} %get-tuple-element.58), channel_id=1, source_target_pairs={{0,1},{1,2},{2,3},{3,4},{4,5},{5,6},{6,7},{8,9},{9,10},{10,11},{11... | collective-permute-start | bytes 49160 | tf_op jit(solution)/shard_map/ppermute | solution.py:14
  80.6 1.3 collective-permute-start.3
  81.9 1.2 fusion.80
  83.2 9.0 %copy.178 = f32[8,8,8,33,16]{3,2,4,1,0:T(8,128)} copy(f32[8,8,8,33,16]{4,2,3,1,0:T(8,128)} %get-tuple-element.64) | data formatting | bytes 2162688 | tf_op jit(solution)/shard_map/jit(_where)/select_n | solution.py:54
  92.3 3.5 reshape.117
  95.9 4.6 %copy.190 = f32[8,8,1,256,16]{4,3,1,0,2:T(8,128)} copy(f32[8,8,1,256,16]{3,4,1,0,2:T(8,128)S(1)} %slice.45) | data formatting | bytes 2097152
  100.5 29.6 %copy.176 = bf16[4,1,10,10,258]{0,1,4,3,2:T(2,128)(2,1)} copy(bf16[4,1,10,10,258]{4,3,2,0,1:T(8,128)(2,1)S(1)} %copy-done.6) | data formatting | bytes 412800 | tf_op jit(solution)/shard_map/broadcast_in_dim | solution.py:35
  130.1 1.0 copy.158
  131.3 0.9 fusion.78
  132.2 0.8 reshape.102
  133.0 2.0 copy.162
  135.2 2.8 fusion.36
  138.3 1.2 fusion.40
  139.5 1.1 convert_reduce_fusion.1
  140.6 2.5 copy.180
  143.3 4.6 %collective-permute-start.4 = (bf16[32,1,4,128]{0,2,3,1:T(4,128)(2,1)S(1)}, bf16[32,1,4,128]{0,2,3,1:T(4,128)(2,1)S(1)}, u32[]{:S(2)}, u32[]{:S(2)}) collective-permute-start(bf16[32,1,4,128]{0,2,3,1:T(4,128)(2,1)S(1)} %get-tuple-element.56), channel_id=1, source_target_pairs={{0,1},{1,2},{2,3},{3,4},{4,5},{5,6},{6,7},{8,9},{9,10},{10,11},{11... | collective-permute-start | bytes 98312 | tf_op jit(solution)/shard_map/ppermute | solution.py:14
  147.9 1.5 collective-permute-start.5
  149.3 1.3 copy.163
  150.6 16.5 %fusion.44 = f32[32,16,3,3,3]{0,1,4,3,2:T(8,128)} fusion(bf16[16,1,6,6,130]{0,1,4,3,2:T(2,128)(2,1)S(1)} %copy.180, bf16[32,1,4,4,128]{0,3,4,2,1:T(4,128)(2,1)} %fusion.40), kind=kOutput, calls=%fused_computation.64 | convolution fusion | flops 56623104 | bytes 336128 | tf_op jit(solution)/shard_map/transpose | solution.py:42
  167.6 0.9 copy.182
  169.1 1.7 reshape.111
  170.8 3.0 copy.170
  173.8 1.0 slice.43
  174.8 3.2 fusion.18
  178.0 0.9 copy.171
  179.0 0.9 copy.186
  180.2 1.0 slice_bitcast_fusion.2
  181.3 7.4 %broadcast_in_dim.50 = f32[16,4,2,4,2,128,2]{0,6,5,4,3,2,1:T(2,128)} broadcast(f32[16,4,4,128]{0,3,2,1:T(8,128)S(1)} %convert_multiply_fusion), dimensions={0,1,3,5} | broadcast | bytes 1179648 | tf_op jit(solution)/shard_map/broadcast_in_dim | solution.py:65
  188.8 5.2 %copy.175 = f32[16,1,8,8,256]{4,0,3,2,1:T(8,128)S(1)} copy(f32[16,1,8,8,256]{0,4,3,2,1:T(8,128)} %bitcast.108) | data formatting | bytes 2097152 | tf_op jit(solution)/shard_map/mul | solution.py:95
  194.2 14.3 %copy.177 = bf16[16,1,8,8,256]{0,1,4,3,2:T(2,128)(2,1)} copy(bf16[16,1,8,8,256]{4,0,3,2,1:T(8,128)(2,1)S(1)} %multiply_convert_fusion) | data formatting | bytes 1048576 | tf_op jit(solution)/shard_map/convert_element_type | solution.py:96
  208.6 8.6 %convert_reduce_fusion = f32[16]{0:T(128)} fusion(f32[1,16,8,8,256]{1,4,3,2,0:T(8,128)} %bitcast.109, f32[8,8,1,256,16]{4,3,1,0,2:T(8,128)} %copy.190), kind=kLoop, calls=%fused_computation.5 | loop fusion | flops 1048560 | bytes 2097216 | tf_op jit(solution)/shard_map/reduce_sum | solution.py:99
  217.2 183.2 %fusion.81 = f32[16,4,3,3,3]{0,1,4,3,2:T(4,128)S(1)} fusion(bf16[4,1,10,10,258]{0,1,4,3,2:T(2,128)(2,1)} %copy.176, bf16[16,1,8,8,256]{0,1,4,3,2:T(2,128)(2,1)S(1)} %copy-done.4), kind=kOutput, calls=%fused_computation.118 | convolution fusion | flops 56623104 | bytes 737600 | tf_op jit(solution)/shard_map/transpose | solution.py:42
  400.4 46.4 %all-reduce.3 = (f32[16,4,3,3,3]{0,1,4,3,2:T(4,128)S(1)}, f32[16]{0:T(128)S(1)}, f32[32,16,3,3,3]{0,1,4,3,2:T(8,128)S(1)}, f32[32]{0:T(128)S(1)}) all-reduce(f32[16,4,3,3,3]{0,1,4,3,2:T(4,128)S(1)} %fusion.81, f32[16]{0:T(128)S(1)} %copy-done.10, ...), channel_id=1, replica_groups=mesh['dp'=4,'space'=8] {'dp','space'}, use_global_device_ids=true, to_apply=%region_1.2 | all-reduce | flops 15600 | bytes 124800 | tf_op jit(solution)/shard_map/psum | solution.py:101
  449.2 0.9 copy.183
  (69 shorter events, 6.2 us)
Async XLA Ops:
  0.6 134.5 %copy-start = (bf16[32,16,3,3,3]{0,1,4,3,2:T(8,128)(2,1)S(1)}, bf16[32,16,3,3,3]{0,1,4,3,2:T(8,128)(2,1)}, u32[]{:S(2)}) copy-start(bf16[32,16,3,3,3]{0,1,4,3,2:T(8,128)(2,1)} %param.9) | copy-start | bytes 82948
  1.4 7.5 %collective-permute-start = (bf16[4,1,8,256]{3,2,1,0:T(8,128)(2,1)S(1)}, bf16[4,1,8,256]{3,2,1,0:T(8,128)(2,1)S(1)}, u32[]{:S(2)}, u32[]{:S(2)}) collective-permute-start(bf16[4,1,8,256]{3,2,1,0:T(8,128)(2,1)S(1)} %get-tuple-element.60), channel_id=1, source_target_pairs={{0,1},{1,2},{2,3},{3,4},{4,5},{5,6},{6,7},{8,9},{9,10},{10,11},{11... | collective-permute-start | bytes 49160 | tf_op jit(solution)/shard_map/ppermute | solution.py:14
  6.3 5.6 %collective-permute-start.1 = (bf16[4,1,8,256]{3,2,1,0:T(8,128)(2,1)S(1)}, bf16[4,1,8,256]{3,2,1,0:T(8,128)(2,1)S(1)}, u32[]{:S(2)}, u32[]{:S(2)}) collective-permute-start(bf16[4,1,8,256]{3,2,1,0:T(8,128)(2,1)S(1)} %get-tuple-element.61), channel_id=1, source_target_pairs={{1,0},{2,1},{3,2},{4,3},{5,4},{6,5},{7,6},{9,8},{10,9},{11,10},{12... | collective-permute-start | bytes 49160 | tf_op jit(solution)/shard_map/ppermute | solution.py:17
  13.3 6.3 %copy-start.12 = (f32[16]{0:T(128)S(1)}, f32[16]{0:T(128)}, u32[]{:S(2)}) copy-start(f32[16]{0:T(128)} %param.8) | copy-start | bytes 196
  13.3 6.3 %copy-start.16 = (bf16[16,4,3,3,3]{0,1,4,3,2:T(4,128)(2,1)S(1)}, bf16[16,4,3,3,3]{0,1,4,3,2:T(4,128)(2,1)}, u32[]{:S(2)}) copy-start(bf16[16,4,3,3,3]{0,1,4,3,2:T(4,128)(2,1)} %param.7) | copy-start | bytes 10372
  13.3 6.3 %copy-start.17 = (pred[8,33]{0,1:T(8,128)(4,1)S(1)}, pred[8,33]{0,1:T(8,128)(4,1)}, u32[]{:S(2)}) copy-start(pred[8,33]{0,1:T(8,128)(4,1)} %constant.43) | copy-start | bytes 796
  57.0 4.9 %copy-start.2 = (f32[8,8,1,264,16]{3,4,1,0,2:T(8,128)}, f32[8,8,1,264,16]{3,4,1,0,2:T(8,128)S(1)}, u32[]{:S(2)}) copy-start(f32[8,8,1,264,16]{3,4,1,0,2:T(8,128)S(1)} %reshape.99) | copy-start | bytes 3244036
  61.9 19.9 %copy-start.8 = (bf16[1,4,8,8,256]{4,3,2,1,0:T(8,128)(2,1)S(1)}, bf16[1,4,8,8,256]{4,3,2,1,0:T(8,128)(2,1)}, u32[]{:S(2)}) copy-start(bf16[1,4,8,8,256]{4,3,2,1,0:T(8,128)(2,1)} %param.6) | copy-start | bytes 393220
  75.6 54.5 %collective-permute-start.2 = (bf16[16,1,4,128]{0,3,2,1:T(8,128)(2,1)}, bf16[16,1,4,128]{0,3,2,1:T(8,128)(2,1)}, u32[]{:S(2)}, u32[]{:S(2)}) collective-permute-start(bf16[16,1,4,128]{0,3,2,1:T(8,128)(2,1)} %get-tuple-element.58), channel_id=1, source_target_pairs={{0,1},{1,2},{2,3},{3,4},{4,5},{5,6},{6,7},{8,9},{9,10},{10,11},{11... | collective-permute-start | bytes 49160 | tf_op jit(solution)/shard_map/ppermute | solution.py:14
  80.6 50.5 %collective-permute-start.3 = (bf16[16,1,4,128]{0,3,2,1:T(8,128)(2,1)}, bf16[16,1,4,128]{0,3,2,1:T(8,128)(2,1)S(1)}, u32[]{:S(2)}, u32[]{:S(2)}) collective-permute-start(bf16[16,1,4,128]{0,3,2,1:T(8,128)(2,1)} %get-tuple-element.59), channel_id=1, source_target_pairs={{1,0},{2,1},{3,2},{4,3},{5,4},{6,5},{7,6},{9,8},{10,9},{11,10},{12... | collective-permute-start | bytes 49160 | tf_op jit(solution)/shard_map/ppermute | solution.py:17
  95.9 4.6 %copy-start.6 = (bf16[4,1,10,10,258]{4,3,2,0,1:T(8,128)(2,1)S(1)}, bf16[4,1,10,10,258]{4,3,2,0,1:T(8,128)(2,1)}, u32[]{:S(2)}) copy-start(bf16[4,1,10,10,258]{4,3,2,0,1:T(8,128)(2,1)} %fusion.80) | copy-start | bytes 619204
  131.1 4.0 copy-start.11
  131.1 4.0 copy-start.18
  138.0 2.7 copy-start.7
  143.3 25.2 %collective-permute-start.4 = (bf16[32,1,4,128]{0,2,3,1:T(4,128)(2,1)S(1)}, bf16[32,1,4,128]{0,2,3,1:T(4,128)(2,1)S(1)}, u32[]{:S(2)}, u32[]{:S(2)}) collective-permute-start(bf16[32,1,4,128]{0,2,3,1:T(4,128)(2,1)S(1)} %get-tuple-element.56), channel_id=1, source_target_pairs={{0,1},{1,2},{2,3},{3,4},{4,5},{5,6},{6,7},{8,9},{9,10},{10,11},{11... | collective-permute-start | bytes 98312 | tf_op jit(solution)/shard_map/ppermute | solution.py:14
  147.9 20.8 %collective-permute-start.5 = (bf16[32,1,4,128]{0,2,3,1:T(4,128)(2,1)S(1)}, bf16[32,1,4,128]{0,2,3,1:T(4,128)(2,1)S(1)}, u32[]{:S(2)}, u32[]{:S(2)}) collective-permute-start(bf16[32,1,4,128]{0,2,3,1:T(4,128)(2,1)S(1)} %get-tuple-element.57), channel_id=1, source_target_pairs={{1,0},{2,1},{3,2},{4,3},{5,4},{6,5},{7,6},{9,8},{10,9},{11,10},{12... | collective-permute-start | bytes 98312 | tf_op jit(solution)/shard_map/ppermute | solution.py:17
  174.8 4.1 copy-start.15
  188.7 5.2 %copy-start.3 = (f32[8,8,1,264,16]{3,4,1,0,2:T(8,128)S(1)}, f32[8,8,1,264,16]{3,4,1,0,2:T(8,128)}, u32[]{:S(2)}) copy-start(f32[8,8,1,264,16]{3,4,1,0,2:T(8,128)} %copy-done.2) | copy-start | bytes 3244036
  188.7 5.2 %copy-start.13 = (f32[16]{0:T(128)S(1)}, f32[16]{0:T(128)}, u32[]{:S(2)}) copy-start(f32[16]{0:T(128)} %param.8) | copy-start | bytes 196
  208.6 8.7 %copy-start.4 = (bf16[16,1,8,8,256]{0,1,4,3,2:T(2,128)(2,1)S(1)}, bf16[16,1,8,8,256]{0,1,4,3,2:T(2,128)(2,1)}, u32[]{:S(2)}) copy-start(bf16[16,1,8,8,256]{0,1,4,3,2:T(2,128)(2,1)} %copy.177) | copy-start | bytes 1572868
  217.2 183.2 %copy-start.9 = (f32[32,16,3,3,3]{0,1,4,3,2:T(8,128)S(1)}, f32[32,16,3,3,3]{0,1,4,3,2:T(8,128)}, u32[]{:S(2)}) copy-start(f32[32,16,3,3,3]{0,1,4,3,2:T(8,128)} %fusion.44) | copy-start | bytes 165892
  217.2 183.2 %copy-start.10 = (f32[16]{0:T(128)S(1)}, f32[16]{0:T(128)}, u32[]{:S(2)}) copy-start(f32[16]{0:T(128)} %convert_reduce_fusion) | copy-start | bytes 196
  217.2 183.2 %copy-start.14 = (f32[32]{0:T(128)S(1)}, f32[32]{0:T(128)}, u32[]{:S(2)}) copy-start(f32[32]{0:T(128)} %get-tuple-element.52) | copy-start | bytes 388
  217.2 232.0 %copy-start.5 = (bf16[1,16,4,4,128]{1,4,3,2,0:T(8,128)(2,1)S(1)}, bf16[1,16,4,4,128]{1,4,3,2,0:T(8,128)(2,1)}, u32[]{:S(2)}) copy-start(bf16[1,16,4,4,128]{1,4,3,2,0:T(8,128)(2,1)} %get-tuple-element.55) | copy-start | bytes 196612
  217.2 232.8 %copy-start.1 = (bf16[32,16,3,3,3]{0,1,4,3,2:T(8,128)(2,1)S(1)}, bf16[32,16,3,3,3]{0,1,4,3,2:T(8,128)(2,1)}, u32[]{:S(2)}) copy-start(bf16[32,16,3,3,3]{0,1,4,3,2:T(8,128)(2,1)} %param.9) | copy-start | bytes 82948
where the time goes:
time: 459 us; the launch traced here: 450 us
  matrix products  231 us (50%)
  local copies, waits for them, and re-layouts  120 us (26%)
  blocking collectives  46.4 us (10%)
  other arithmetic  30.4 us (7%)
  starting transfers between devices  18.4 us (4%)
    transpose x2, matrix products, kernel_grad(): return result.transpose(1, 0, 2, 3, 4)  200 us
    psum x1, blocking collectives, shards(): first_terms = lax.psum((first_terms[0], first_terms[1]), ('dp', 'space'))  46.4 us
    conv_general_dilated x15, local copies, waits for them, and re-layouts, convolve(): lax.conv_general_dilated(padded[None], kernel, (1, 1, 1), 'VALID', dimens...  32.9 us
    broadcast_in_dim x2, local copies, waits for them, and re-layouts, kernel_grad(): padded[:, None]  32.2 us
    conv_general_dilated x3, matrix products, convolve(): lax.conv_general_dilated(padded[None], kernel, (1, 1, 1), 'VALID', dimens...  31.4 us
    ppermute x3, starting transfers between devices, with_halo(): lax.ppermute(lax.slice_in_dim(block, block.shape[dim] - width, None, axis...  14.4 us
    convert_element_type x1, local copies, waits for them, and re-layouts, shards(): delta_one = (spread_up(stored_grad.astype(jnp.float32)) * 0.125 * rectify...  14.3 us
    reduce_sum x1, other arithmetic, mean_pool(): return jnp.sum(blocks, axis=(2, 4, 6)) * 0.125  12.8 us
  transfers between devices with their start and end apart: 6, of which 1 were waited for; matrix products, arithmetic and copies ran while one was open for 15% of the time, Pallas kernels for 0%

commit v1 on v0

v1 whole, which is shorter than its diff:
```python
import functools
import math

import jax
import jax.numpy as jnp
import numpy as np
from jax import lax
from jax.experimental import pallas as pl
from jax.experimental.pallas import tpu as pltpu
from jax.sharding import PartitionSpec as P

BF = jnp.bfloat16
F32 = jnp.float32
MESH = pl.DeviceIdType.MESH
LANES = 128
RIM = 48
TILES = 16


def tap_choice():
    table = np.zeros((2, 2, 3, 4, 4, 4, 128), np.float32)
    for dd in range(2):
        for wpar in range(2):
            for kh in range(3):
                for s in range(4):
                    for dz in range(4):
                        kd, kw = dz - dd, s - wpar
                        if 0 <= kd < 3 and 0 <= kw < 3:
                            for i in range(4):
                                table[dd, wpar, kh, s, i, dz, ((kd * 3 + kh) * 3 + kw) * 4 + i] = 1
    return table.reshape(4 * 192, 128)


def iota(shape, dim):
    return lax.broadcasted_iota(jnp.int32, shape, dim)


def dot(a, b):
    return jnp.dot(a, b, preferred_element_type=F32)


def dot_nt(a, b):
    return lax.dot_general(a, b, (((1,), (1,)), ((), ())), preferred_element_type=F32)


def column(row, count):
    return jnp.sum(
        jnp.where(iota((count, count), 0) == iota((count, count), 1), row, 0.0),
        axis=1,
        keepdims=True,
    )


def fold(values, steps):
    for step in steps:
        values = values + pltpu.roll(values, step, axis=values.ndim - 1)
    return values


def kernel(
    dp_n, space_n, scale_one, scale_two,
    vol, cot, f1, f2, b1, b2, choice,
    act_out, pg_out, g1_out, s1_out, g2_out, s2_out,
    raw, cots, cotf, shifted, pooled, slopes, errors_two, errors_one, pgf, w1, w2, w2t,
    stack, terms, landed, across, total,
    halo_send, halo_recv, rs_send, rs_recv, dp_send, dp_recv, ag_send, ag_recv,
):
    me = lax.axis_index("space")
    mine = lax.axis_index("dp")
    first = me == 0
    last = me == space_n - 1

    barrier = pltpu.get_barrier_semaphore()
    for k in range(1, space_n):
        pl.semaphore_signal(
            barrier, inc=1, device_id={"space": lax.rem(me + k, space_n)}, device_id_type=MESH
        )
    for k in range(1, dp_n):
        pl.semaphore_signal(
            barrier, inc=1, device_id={"dp": lax.rem(mine + k, dp_n)}, device_id_type=MESH
        )

    cotf[...] = cot[...].reshape(512, LANES).astype(F32)
    for d in range(4):
        for hq in range(4):
            cots[pl.ds((1 + d) * 128 + hq * 32, 32), :] = cotf[
                pl.ds(d * 4 + hq, 32, stride=16), :
            ].astype(BF)
    raw[:, RIM : RIM + 64, :] = vol[...]

    @pl.when(first)
    def _():
        raw[:, 0:RIM, :] = jnp.zeros((4, RIM, 256), BF)
        cots[0:128, :] = jnp.zeros((128, LANES), BF)

    @pl.when(last)
    def _():
        raw[:, RIM + 64 :, :] = jnp.zeros((4, RIM, 256), BF)
        cots[640:768, :] = jnp.zeros((128, LANES), BF)

    pl.semaphore_wait(barrier, space_n - 1 + dp_n - 1)

    right = lax.rem(me + 1, space_n)
    left = lax.rem(me + space_n - 1, space_n)

    def halo(which):
        src, dst, to = (
            (raw.at[:, 64 : 64 + RIM], raw.at[:, 0:RIM], right),
            (raw.at[:, RIM : 2 * RIM], raw.at[:, RIM + 64 : 2 * RIM + 64], left),
            (cots.at[512:640], cots.at[0:128], right),
            (cots.at[128:256], cots.at[640:768], left),
        )[which]
        return pltpu.make_async_remote_copy(
            src_ref=src,
            dst_ref=dst,
            send_sem=halo_send.at[which],
            recv_sem=halo_recv.at[which],
            device_id={"space": to},
            device_id_type=MESH,
        )

    @pl.when(jnp.logical_not(last))
    def _():
        halo(0).start()
        halo(2).start()

    @pl.when(jnp.logical_not(first))
    def _():
        halo(1).start()
        halo(3).start()

    lane = iota((64, 512), 1)
    group = iota((64, 512), 0)
    spread = (
        (lane % 16 == group % 16) & (lane // 256 == group // 32) & ((lane // 64) % 2 == (group // 16) % 2)
    ).astype(F32).astype(BF)
    picked = dot(choice[...], f1[...]).astype(BF)
    rows = jnp.concatenate([picked[g * 192 : (g + 1) * 192] for g in range(4)], axis=1)
    rows = dot(rows, spread)
    lane8 = iota((8, 512), 1)
    reach = iota((8, 512), 0) - (2 * ((lane8 // 16) % 4) + (lane8 // 128) % 2) + 1
    near = [reach == kh for kh in range(3)]
    matrix = jnp.zeros((64, 8, 512), F32)
    for kh in range(3):
        piece = rows[kh * 64 : (kh + 1) * 64].reshape(64, 1, 512)
        matrix = jnp.where(near[kh][None], piece, matrix)
    w1[...] = matrix.reshape(512, 512).T.astype(BF)

    tile4 = (iota((32, 128), 0) == iota((32, 128), 1) % 32).astype(F32).astype(BF)
    wide = dot(f2[...], tile4)
    group4 = iota((16, 128), 1) // 32
    parts = []
    for kd in range(3):
        for kw in range(3):
            for hq in range(4):
                block = jnp.zeros((16, 128), F32)
                for kh in range(3):
                    if 0 <= hq - kh + 1 < 4:
                        tap = (kd * 3 + kh) * 3 + kw
                        block = jnp.where(group4 == hq - kh + 1, wide[tap * 16 : tap * 16 + 16], block)
                parts.append(block)
    joined = jnp.concatenate(parts, axis=0)
    w2t[...] = joined.astype(BF)
    w2[...] = joined.T.astype(BF)

    bias_one = column(b1[...], 16)
    bias_two = column(b2[...], 32)
    take = iota((256, 512), 1)
    sample = (iota((256, 512), 0) == 2 * (take % 128) - 1 + take // 128).astype(F32).astype(BF)

    @pl.when(jnp.logical_not(last))
    def _():
        halo(1).wait_recv()

    @pl.when(jnp.logical_not(first))
    def _():
        halo(0).wait_recv()

    columns = dot(raw[...].reshape(4 * 160, 256), sample).reshape(4, 160, 512)[:, 8:152]
    for s in range(4):
        shifted[s * 4 : s * 4 + 4] = columns[:, :, s * 128 : (s + 1) * 128].astype(BF)

    lane64 = iota((64, 128), 1)

    def window(p):
        return shifted[:, pl.ds(pl.multiple_of(p * 16, 16), 32), :].reshape(512, LANES)

    def layer_one(p, carry):
        linear = dot(w1[...], window(p)).reshape(32, 16, LANES) + bias_one[None]
        linear = linear.reshape(8, 64, LANES)
        slope = jnp.where(linear > 0, 1.0, 0.3)
        slopes[p] = slope
        mean = jnp.sum(linear * slope, axis=0) * 0.125
        outside = (first & (p < 2)) | (last & (p > 5))
        mean = jnp.where(outside, 0.0, mean)
        base = pl.multiple_of(p * 192, 16)
        pooled[pl.ds(base, 64), :] = jnp.where(lane64 == 0, 0.0, pltpu.roll(mean, 1, axis=1)).astype(BF)
        pooled[pl.ds(base + 64, 64), :] = mean.astype(BF)
        pooled[pl.ds(base + 128, 64), :] = jnp.where(
            lane64 == 127, 0.0, pltpu.roll(mean, 127, axis=1)
        ).astype(BF)
        return carry

    lax.fori_loop(0, 8, layer_one, 0)

    @pl.when(jnp.logical_not(last))
    def _():
        halo(3).wait_recv()

    @pl.when(jnp.logical_not(first))
    def _():
        halo(2).wait_recv()

    for j in range(6):
        linear = dot(w2[...], pooled[j * 192 : j * 192 + 576, :]).reshape(4, 32, LANES)
        linear = (linear + bias_two[None]).reshape(128, LANES)
        slope = jnp.where(linear > 0, 1.0, 0.3)
        errors_two[j * 128 : (j + 1) * 128, :] = (
            cots[j * 128 : (j + 1) * 128, :].astype(F32) * slope
        ).astype(BF)
        if 1 <= j <= 4:
            out = linear * slope
            for hq in range(4):
                cotf[pl.ds((j - 1) * 4 + hq, 32, stride=16), :] = out[hq * 32 : (hq + 1) * 32]
    act_out[...] = cotf[...].astype(BF).reshape(32, 16, LANES)

    own = jnp.concatenate(
        [errors_two[j * 128 : (j + 1) * 128, :] for j in range(1, 5)], axis=1
    )
    near_in = jnp.concatenate(
        [pooled[j * 192 : j * 192 + 576, :] for j in range(1, 5)], axis=1
    )
    near_in = jnp.concatenate([near_in, jnp.ones((16, 512), BF)], axis=0)
    outer = dot_nt(near_in, own)
    taps = []
    for kd in range(3):
        for kh in range(3):
            for kw in range(3):
                block = jnp.zeros((16, 128), F32)
                for hq in range(4):
                    if 0 <= hq - kh + 1 < 4:
                        at = ((kd * 3 + kw) * 4 + hq) * 16
                        block = jnp.where(group4 == hq - kh + 1, outer[at : at + 16], block)
                taps.append(fold(block, (64, 32)))
    taps.append(fold(outer[576:592], (64, 32)))
    for q in range(7):
        block = taps[4 * q]
        for slot in range(1, 4):
            block = jnp.where(group4 == slot, taps[4 * q + slot], block)
        terms[2 * q] = block[0:8]
        terms[2 * q + 1] = block[8:16]

    back = jnp.concatenate([w2t[kd * 192 : (kd + 1) * 192, :] for kd in (2, 1, 0)], axis=1)
    for q in range(4):
        three = dot(back, errors_two[q * 128 : q * 128 + 384, :])
        grad = three[64:128]
        grad = grad + jnp.where(lane64 == 127, 0.0, pltpu.roll(three[0:64], 127, axis=1))
        grad = grad + jnp.where(lane64 == 0, 0.0, pltpu.roll(three[128:192], 1, axis=1))
        grad = grad.astype(BF).astype(F32)
        for hq in range(4):
            pgf[pl.ds(q * 4 + hq, 16, stride=16), :] = grad[hq * 16 : (hq + 1) * 16]
        errors_one[:, q * 128 : (q + 1) * 128] = (
            ((grad * 0.125)[None] * slopes[q + 2]).astype(BF).reshape(512, LANES)
        )
    pg_out[...] = pgf[...].astype(BF).reshape(16, 16, LANES)

    near_in = jnp.concatenate([window(p) for p in range(2, 6)], axis=1)
    near_in = jnp.concatenate([near_in, jnp.ones((16, 512), BF)], axis=0)
    outer = dot_nt(near_in, errors_one[...])
    body = outer[0:512].reshape(4, 4, 4, 8, 512)
    low = iota((4, 3, 8, 128), 3) < 64
    for kh in range(3):
        summed = jnp.zeros((4, 4, 3, 8, 128), F32)
        for part in range(4):
            dd = part // 2
            cut = body[:, :, dd : dd + 3, :, part * 128 : (part + 1) * 128]
            mask = near[kh][:, part * 128 : (part + 1) * 128]
            summed = summed + jnp.where(mask[None, None, None], cut, 0.0)
        for kw in range(3):
            both = jnp.where(low, summed[kw], summed[kw + 1])
            for kd in range(3):
                tap = (kd * 3 + kh) * 3 + kw
                stack[tap * 32 : tap * 32 + 32, :] = both[:, kd].reshape(32, LANES)
    ones = outer[512:520]
    ones = ones[:, 0:128] + ones[:, 128:256] + ones[:, 256:384] + ones[:, 384:512]
    stack[864:872, :] = jnp.where(iota((8, 128), 0) == 0, ones, 0.0)
    stack[872:896, :] = jnp.zeros((24, 128), F32)
    gather = (iota((112, 896), 0) == iota((112, 896), 1) // 8).astype(F32).astype(BF)
    whole = stack[...]
    high = whole.astype(BF)
    rest = (whole - high.astype(F32)).astype(BF)
    reduced = fold(dot(gather, high) + dot(gather, rest), (64, 32, 16))
    group8 = iota((8, 128), 1) // 16
    for half in range(2):
        block = jnp.zeros((8, 128), F32)
        for slot in range(8):
            v = half * 8 + slot
            if v < 14:
                block = jnp.where(group8 == slot, reduced[v * 8 : v * 8 + 8], block)
        terms[14 + half] = block

    share = TILES // space_n

    def scatter(k):
        to = lax.rem(me + k, space_n)
        return pltpu.make_async_remote_copy(
            src_ref=terms.at[pl.ds(to * share, share)],
            dst_ref=landed.at[k - 1],
            send_sem=rs_send.at[k - 1],
            recv_sem=rs_recv.at[k - 1],
            device_id={"space": to},
            device_id_type=MESH,
        )

    for k in range(1, space_n):
        scatter(k).start()
    sums = terms[pl.ds(me * share, share)]
    for k in range(1, space_n):
        scatter(k).wait_recv()
        sums = sums + landed[k - 1]
    across[mine] = sums

    def exchange(k):
        to = lax.rem(mine + k, dp_n)
        return pltpu.make_async_remote_copy(
            src_ref=across.at[mine],
            dst_ref=across.at[mine],
            send_sem=dp_send.at[k - 1],
            recv_sem=dp_recv.at[k - 1],
            device_id={"dp": to},
            device_id_type=MESH,
        )

    def arrival(k):
        source = lax.rem(mine + dp_n - k, dp_n)
        return pltpu.make_async_remote_copy(
            src_ref=across.at[source],
            dst_ref=across.at[source],
            send_sem=dp_send.at[k - 1],
            recv_sem=dp_recv.at[k - 1],
            device_id={"dp": source},
            device_id_type=MESH,
        )

    for k in range(1, dp_n):
        exchange(k).start()
    for k in range(1, dp_n):
        arrival(k).wait_recv()
    sums = across[0]
    for k in range(1, dp_n):
        sums = sums + across[k]
    total[pl.ds(me * share, share)] = sums

    def spread_out(k, source):
        return pltpu.make_async_remote_copy(
            src_ref=total.at[pl.ds(source * share, share)],
            dst_ref=total.at[pl.ds(source * share, share)],
            send_sem=ag_send.at[k - 1],
            recv_sem=ag_recv.at[k - 1],
            device_id={"space": lax.rem(me + k, space_n)},
            device_id_type=MESH,
        )

    for k in range(1, space_n):
        spread_out(k, me).start()
    for k in range(1, space_n):
        spread_out(k, lax.rem(me + space_n - k, space_n)).wait_recv()

    for q in range(7):
        block = jnp.concatenate([total[2 * q], total[2 * q + 1]], axis=0) * scale_two
        for slot in range(4):
            tap = 4 * q + slot
            turned = block if slot == 0 else pltpu.roll(block, 128 - 32 * slot, axis=1)
            if tap < 27:
                g2_out[tap * 16 : tap * 16 + 16, :] = turned[:, 0:32]
            else:
                s2_out[...] = turned[0:1, 0:32]
    for v in range(14):
        block = total[14 + v // 8] * scale_one
        slot = v % 8
        turned = block if slot == 0 else pltpu.roll(block, 128 - 16 * slot, axis=1)
        if v < 13:
            g1_out[v * 8 : v * 8 + 8, :] = turned[:, 0:16]
        else:
            g1_out[104:108, :] = turned[0:4, 0:16]
            s1_out[...] = turned[4:5, 0:16]

    for k in range(1, space_n):
        scatter(k).wait_send()
        spread_out(k, me).wait_send()
    for k in range(1, dp_n):
        exchange(k).wait_send()

    @pl.when(jnp.logical_not(last))
    def _():
        halo(0).wait_send()
        halo(2).wait_send()

    @pl.when(jnp.logical_not(first))
    def _():
        halo(1).wait_send()
        halo(3).wait_send()


def shards(dp_n, space_n, volume, first_filters, first_biases, second_filters, second_biases, cotangent):
    _, c_in, planes, high, wide = volume.shape
    c1, c2 = first_filters.shape[0], second_filters.shape[0]
    assert (c_in, planes, high, wide, c1, c2) == (4, 8, 8, 256, 16, 32)
    assert TILES % space_n == 0
    count_one = dp_n * space_n * planes * high * wide
    scale_one = 1.0 / math.sqrt(count_one)
    scale_two = 1.0 / math.sqrt(count_one / 8)
    share = TILES // space_n
    f1 = first_filters.transpose(2, 3, 4, 1, 0).reshape(108, 16)
    f1 = jnp.pad(f1, ((0, 20), (0, 0)))
    f2 = second_filters.transpose(2, 3, 4, 1, 0).reshape(432, 32)
    vmem = pl.BlockSpec(memory_space=pltpu.VMEM)
    dma = pltpu.SemaphoreType.DMA
    act, pg, g1, s1, g2, s2 = pl.pallas_call(
        functools.partial(kernel, dp_n, space_n, scale_one, scale_two),
        out_shape=(
            jax.ShapeDtypeStruct((32, 16, 128), BF),
            jax.ShapeDtypeStruct((16, 16, 128), BF),
            jax.ShapeDtypeStruct((108, 16), F32),
            jax.ShapeDtypeStruct((1, 16), F32),
            jax.ShapeDtypeStruct((432, 32), F32),
            jax.ShapeDtypeStruct((1, 32), F32),
        ),
        in_specs=[vmem] * 7,
        out_specs=(vmem,) * 6,
        scratch_shapes=[
            pltpu.VMEM((4, 2 * RIM + 64, 256), BF),
            pltpu.VMEM((768, 128), BF),
            pltpu.VMEM((512, 128), F32),
            pltpu.VMEM((16, 144, 128), BF),
            pltpu.VMEM((8 * 192, 128), BF),
            pltpu.VMEM((8, 8, 64, 128), F32),
            pltpu.VMEM((768, 128), BF),
            pltpu.VMEM((512, 512), BF),
            pltpu.VMEM((256, 128), F32),
            pltpu.VMEM((512, 512), BF),
            pltpu.VMEM((128, 576), BF),
            pltpu.VMEM((576, 128), BF),
            pltpu.VMEM((896, 128), F32),
            pltpu.VMEM((TILES, 8, 128), F32),
            pltpu.VMEM((space_n - 1, share, 8, 128), F32),
            pltpu.VMEM((dp_n, share, 8, 128), F32),
            pltpu.VMEM((TILES, 8, 128), F32),
            dma((4,)),
            dma((4,)),
            dma((space_n - 1,)),
            dma((space_n - 1,)),
            dma((dp_n - 1,)),
            dma((dp_n - 1,)),
            dma((space_n - 1,)),
            dma((space_n - 1,)),
        ],
        compiler_params=pltpu.CompilerParams(
            collective_id=0, has_side_effects=True, vmem_limit_bytes=40 * 1024 * 1024
        ),
    )(
        volume.reshape(4, 64, 256),
        cotangent.reshape(32, 16, 128),
        f1,
        f2,
        first_biases.reshape(1, 16),
        second_biases.reshape(1, 32),
        jnp.asarray(tap_choice(), BF),
    )
    return (
        act.reshape(1, 32, 4, 4, 128),
        pg.reshape(1, 16, 4, 4, 128),
        g1.reshape(3, 3, 3, 4, 16).transpose(4, 3, 0, 1, 2),
        s1.reshape(16),
        g2.reshape(3, 3, 3, 16, 32).transpose(4, 3, 0, 1, 2),
        s2.reshape(32),
    )


def solution(mesh):
    placed = (
        P("dp", None, "space", None, None),
        P(),
        P(),
        P(),
        P(),
        P("dp", None, "space", None, None),
    )
    return jax.shard_map(
        functools.partial(shards, mesh.shape["dp"], mesh.shape["space"]),
        mesh=mesh,
        in_specs=placed,
        out_specs=(
            P("dp", None, "space", None, None),
            P("dp", None, "space", None, None),
            P(),
            P(),
            P(),
            P(),
        ),
        check_vma=False,
    )
```

time: 459 us -> 38 us (0.08); the launches traced: 450 us -> 37.8 us
  matrix products: 231 us -> 0 us
  local copies, waits for them, and re-layouts: 120 us -> 7.83 us
  blocking collectives: 46.4 us -> 0 us
  other arithmetic: 30.4 us -> 0 us
  Pallas kernels: 0 us -> 29.3 us
  starting transfers between devices: 18.4 us -> 0 us
    transpose x2 -> x0, matrix products: 200 us -> none  [kernel_grad(): return result.transpose(1, 0, 2, 3, 4)]
    psum x1 -> x0, blocking collectives: 46.4 us -> none  [shards(): first_terms = lax.psum((first_terms[0], first_terms[1]), ('dp', 'space'))]
    broadcast_in_dim x6 -> x0, local copies, waits for them, and re-layouts: 39.8 us -> none  [the longest x2 32.2 us: kernel_grad(): padded[:, None]]
    conv_general_dilated x15 -> x0, local copies, waits for them, and re-layouts: 32.9 us -> none  [convolve(): lax.conv_general_dilated(padded[None], kernel, (1, 1, 1), 'VALID', dimens...]
    conv_general_dilated x3 -> x0, matrix products: 31.4 us -> none  [convolve(): lax.conv_general_dilated(padded[None], kernel, (1, 1, 1), 'VALID', dimens...]
    pallas_call x0 -> x1, Pallas kernels: none -> 29.3 us  [shards(): pl.pallas_call(functools.partial(kernel, dp_n, space_n, scale_one, scale_...]
    reduce_sum x3 -> x0, other arithmetic: 22.6 us -> none  [the longest x1 12.8 us: mean_pool(): return jnp.sum(blocks, axis=(2, 4, 6)) * 0.125]
    ppermute x6 -> x0, starting transfers between devices: 18.4 us -> none  [the longest x3 14.4 us: with_halo(): lax.ppermute(lax.slice_in_dim(block, block.shape[dim] - width, None, axis...]
  transfers between devices with their start and end apart: 6 -> 0, of which waited for: 1 -> 0; matrix products, arithmetic and copies ran while one was open for 15% -> 0% of each run, Pallas kernels for 0% -> 0%
where the time goes in v1:
time: 38 us; the launch traced here: 37.8 us
  Pallas kernels  29.3 us (77%)
  local copies, waits for them, and re-layouts  7.83 us (21%)
  between operations  0.68 us (2%)
    pallas_call x1, Pallas kernels, shards(): pl.pallas_call(functools.partial(kernel, dp_n, space_n, scale_one, scale_...  29.3 us
    unnamed x17, local copies, waits for them, and re-layouts  6.38 us
    reshape x1, local copies, waits for them, and re-layouts, shards(): f1 = first_filters.transpose(2, 3, 4, 1, 0).reshape(108, 16)  0.8 us

profile of v1, /device:TPU:0, one launch (start us, length us, event | category | flops | bytes accessed | tf_op | source)
XLA Modules:
  0.0 37.8 jit_solution(17746349555061583553)
XLA Ops:
  0.6 0.0 copy-start.3
  0.6 0.8 %reshape.50 = bf16[108,16]{1,0:T(8,128)(2,1)S(1)} reshape(bf16[3,3,3,4,16]{4,3,2,1,0:T(4,128)(2,1)} %bitcast.27) | data formatting | bytes 6912 | tf_op jit(solution)/shard_map/reshape | solution.py:414
  1.4 0.0 copy-start.4
  1.5 0.0 copy-start.5
  1.5 0.1 copy-done.3
  1.5 0.6 %copy-done.4 = f32[16]{0:T(128)S(1)} copy-done((f32[16]{0:T(128)S(1)}, f32[16]{0:T(128)}, u32[]{:S(2)}) %copy-start.4) | copy-done | bytes 88
  2.1 0.0 copy-done.5
  2.1 0.0 copy-start
  2.1 0.9 %copy-done = bf16[768,128]{1,0:T(8,128)(2,1)S(1)} copy-done((bf16[768,128]{1,0:T(8,128)(2,1)S(1)}, bf16[768,128]{1,0:T(8,128)(2,1)}, u32[]{:S(2)}) %copy-start) | copy-done | bytes 196632
  3.1 0.0 copy-start.1
  3.1 0.9 %copy-done.1 = bf16[1,4,8,8,256]{4,3,2,1,0:T(8,128)(2,1)S(1)} copy-done((bf16[1,4,8,8,256]{4,3,2,1,0:T(8,128)(2,1)S(1)}, bf16[1,4,8,8,256]{4,3,2,1,0:T(8,128)(2,1)}, u32[]{:S(2)}) %copy-start.1) | copy-done | bytes 131096
  4.0 0.0 copy-start.2
  4.0 0.9 %copy-done.2 = bf16[1,32,4,4,128]{4,3,2,1,0:T(4,128)(2,1)S(1)} copy-done((bf16[1,32,4,4,128]{4,3,2,1,0:T(4,128)(2,1)S(1)}, bf16[1,32,4,4,128]{4,3,2,1,0:T(4,128)(2,1)}, u32[]{:S(2)}) %copy-start.2) | copy-done | bytes 131096
  4.9 29.3 %shard_map.118 = (bf16[32,16,128]{2,1,0:T(8,128)(2,1)S(1)}, bf16[16,16,128]{2,1,0:T(8,128)(2,1)S(1)}, f32[108,16]{1,0:T(8,128)S(1)}, f32[1,16]{1,0:T(1,128)S(1)}...) custom-call(bf16[4,64,256]{2,1,0:T(8,128)(2,1)S(1)} %bitcast.18, bf16[32,16,128]{2,1,0:T(8,128)(2,1)S(1)} %bitcast.19, ...), custom_call_target="tpu_custom_call" | custom-call | tf_op jit(solution)/shard_map/pallas_call | solution.py:419
  34.1 0.6 %reshape.56 = f32[3,3,3,4,16]{4,3,2,1,0:T(4,128)} reshape(f32[108,16]{1,0:T(8,128)S(1)} %get-tuple-element.14) | data formatting | bytes 13824 | tf_op jit(solution)/shard_map/reshape | solution.py:473
  34.8 0.7 %copy.18 = bf16[1,32,4,4,128]{4,3,2,1,0:T(4,128)(2,1)} copy(bf16[1,32,4,4,128]{4,3,2,1,0:T(4,128)(2,1)S(1)} %bitcast.17) | data formatting | bytes 262144
  35.4 0.6 %copy.19 = bf16[1,16,4,4,128]{4,3,2,1,0:T(4,128)(2,1)} copy(bf16[1,16,4,4,128]{4,3,2,1,0:T(4,128)(2,1)S(1)} %bitcast.21) | data formatting | bytes 131072
  36.1 0.5 %copy.20 = f32[16]{0:T(128)} copy(f32[16]{0:T(128)S(1)} %bitcast.25) | data formatting | bytes 128
  36.6 0.7 %copy.21 = f32[32,16,3,3,3]{0,1,4,3,2:T(8,128)} copy(f32[32,16,3,3,3]{0,1,4,3,2:T(8,128)S(1)} %bitcast.16) | data formatting | bytes 110592
  37.3 0.5 %copy.22 = f32[32]{0:T(128)} copy(f32[32]{0:T(128)S(1)} %bitcast.24) | data formatting | bytes 256
  (1 shorter events, 0.0 us)
Async XLA Ops:
  0.6 0.9 %copy-start.3 = (bf16[32,16,3,3,3]{0,1,4,3,2:T(8,128)(2,1)S(1)}, bf16[32,16,3,3,3]{0,1,4,3,2:T(8,128)(2,1)}, u32[]{:S(2)}) copy-start(bf16[32,16,3,3,3]{0,1,4,3,2:T(8,128)(2,1)} %param.10) | copy-start | bytes 82948
  1.4 0.7 %copy-start.4 = (f32[16]{0:T(128)S(1)}, f32[16]{0:T(128)}, u32[]{:S(2)}) copy-start(f32[16]{0:T(128)} %param.9) | copy-start | bytes 196
  1.5 0.7 %copy-start.5 = (f32[32]{0:T(128)S(1)}, f32[32]{0:T(128)}, u32[]{:S(2)}) copy-start(f32[32]{0:T(128)} %param.11) | copy-start | bytes 388
  2.1 0.9 %copy-start = (bf16[768,128]{1,0:T(8,128)(2,1)S(1)}, bf16[768,128]{1,0:T(8,128)(2,1)}, u32[]{:S(2)}) copy-start(bf16[768,128]{1,0:T(8,128)(2,1)} %constant.5.clone.choice) | copy-start | bytes 589828
  3.1 0.9 %copy-start.1 = (bf16[1,4,8,8,256]{4,3,2,1,0:T(8,128)(2,1)S(1)}, bf16[1,4,8,8,256]{4,3,2,1,0:T(8,128)(2,1)}, u32[]{:S(2)}) copy-start(bf16[1,4,8,8,256]{4,3,2,1,0:T(8,128)(2,1)} %param.7) | copy-start | bytes 393220
  4.0 0.9 %copy-start.2 = (bf16[1,32,4,4,128]{4,3,2,1,0:T(4,128)(2,1)S(1)}, bf16[1,32,4,4,128]{4,3,2,1,0:T(4,128)(2,1)}, u32[]{:S(2)}) copy-start(bf16[1,32,4,4,128]{4,3,2,1,0:T(4,128)(2,1)} %param.12) | copy-start | bytes 393220

commit v2 on v1

v2 whole, which is shorter than its diff:
```python
import functools
import math

import jax
import jax.numpy as jnp
import numpy as np
from jax import lax
from jax.experimental import pallas as pl
from jax.experimental.pallas import tpu as pltpu
from jax.sharding import PartitionSpec as P

BF = jnp.bfloat16
F32 = jnp.float32
MESH = pl.DeviceIdType.MESH
LANES = 128
RIM = 48
VMEM_LIMIT = 60 * 1024 * 1024
TILES = 16


def tap_choice():
    table = np.zeros((2, 2, 3, 4, 4, 4, 128), np.float32)
    for dd in range(2):
        for wpar in range(2):
            for kh in range(3):
                for s in range(4):
                    for dz in range(4):
                        kd, kw = dz - dd, s - wpar
                        if 0 <= kd < 3 and 0 <= kw < 3:
                            for i in range(4):
                                table[dd, wpar, kh, s, i, dz, ((kd * 3 + kh) * 3 + kw) * 4 + i] = 1
    return table.reshape(4 * 192, 128)


def iota(shape, dim):
    return lax.broadcasted_iota(jnp.int32, shape, dim)


def dot(a, b):
    return jnp.dot(a, b, preferred_element_type=F32)


def dot_nt(a, b):
    return lax.dot_general(a, b, (((1,), (1,)), ((), ())), preferred_element_type=F32)


def column(row, count):
    return jnp.sum(
        jnp.where(iota((count, count), 0) == iota((count, count), 1), row, 0.0),
        axis=1,
        keepdims=True,
    )


def fold(values, steps):
    for step in steps:
        values = values + pltpu.roll(values, step, axis=values.ndim - 1)
    return values


def kernel(
    dp_n, space_n,
    vol, cot, f1, f2, b1, b2, choice,
    act_out, pg_out, sums_out,
    raw, cotb, f1b, f1f, f2b, b1b, b2b, chosen,
    cots, cotf, shifted, pooled, slopes, errors_two, errors_one, pgf, w1, w2, w2t,
    stack, terms, landed, across, total, late, late_space, late_dp,
    act_here, pg_here, sums_here, out_sem, in_sem, halo_send, halo_recv, rs_send, rs_recv, dp_send, dp_recv, ag_send, ag_recv,
    ls_send, ls_recv, ld_send, ld_recv,
):
    me = lax.axis_index("space")
    mine = lax.axis_index("dp")
    first = me == 0
    last = me == space_n - 1

    barrier = pltpu.get_barrier_semaphore()
    for k in range(1, space_n):
        pl.semaphore_signal(
            barrier, inc=1, device_id={"space": lax.rem(me + k, space_n)}, device_id_type=MESH
        )
    for k in range(1, dp_n):
        pl.semaphore_signal(
            barrier, inc=1, device_id={"dp": lax.rem(mine + k, dp_n)}, device_id_type=MESH
        )
    loads = [
        pltpu.make_async_copy(src, dst, in_sem.at[n])
        for n, (src, dst) in enumerate(
            (
                (cot, cotb),
                (f1, f1b),
                (choice, chosen),
                (f2, f2b),
                (b1, b1b),
                (b2, b2b),
                (vol, raw.at[:, RIM : RIM + 64]),
            )
        )
    ]
    for load in loads:
        load.start()

    @pl.when(first)
    def _():
        raw[:, 0:RIM, :] = jnp.zeros((4, RIM, 256), BF)
        cots[0:128, :] = jnp.zeros((128, LANES), BF)

    @pl.when(last)
    def _():
        raw[:, RIM + 64 :, :] = jnp.zeros((4, RIM, 256), BF)
        cots[640:768, :] = jnp.zeros((128, LANES), BF)

    right = lax.rem(me + 1, space_n)
    left = lax.rem(me + space_n - 1, space_n)

    def halo(which):
        src, dst, to = (
            (vol.at[:, 16:64], raw.at[:, 0:RIM], right),
            (vol.at[:, 0:RIM], raw.at[:, RIM + 64 : 2 * RIM + 64], left),
            (cots.at[512:640], cots.at[0:128], right),
            (cots.at[128:256], cots.at[640:768], left),
        )[which]
        return pltpu.make_async_remote_copy(
            src_ref=src,
            dst_ref=dst,
            send_sem=halo_send.at[which],
            recv_sem=halo_recv.at[which],
            device_id={"space": to},
            device_id_type=MESH,
        )

    pl.semaphore_wait(barrier, space_n - 1 + dp_n - 1)

    @pl.when(jnp.logical_not(last))
    def _():
        halo(0).start()

    @pl.when(jnp.logical_not(first))
    def _():
        halo(1).start()

    loads[0].wait()
    cotf[...] = cotb[...].reshape(512, LANES).astype(F32)
    for d in range(4):
        for hq in range(4):
            cots[pl.ds((1 + d) * 128 + hq * 32, 32), :] = cotf[
                pl.ds(d * 4 + hq, 32, stride=16), :
            ].astype(BF)

    @pl.when(jnp.logical_not(last))
    def _():
        halo(2).start()

    @pl.when(jnp.logical_not(first))
    def _():
        halo(3).start()

    for load in loads[1:]:
        load.wait()
    f1f[104:128, :] = jnp.zeros((24, 16), F32)
    for tap in range(27):
        f1f[tap * 4 : tap * 4 + 4, :] = f1b[tap].astype(F32)

    lane = iota((64, 512), 1)
    group = iota((64, 512), 0)
    spread = (
        (lane % 16 == group % 16) & (lane // 256 == group // 32) & ((lane // 64) % 2 == (group // 16) % 2)
    ).astype(F32).astype(BF)
    picked = dot(chosen[...], f1f[...].astype(BF)).astype(BF)
    rows = jnp.concatenate([picked[g * 192 : (g + 1) * 192] for g in range(4)], axis=1)
    rows = dot(rows, spread)
    lane8 = iota((8, 512), 1)
    reach = iota((8, 512), 0) - (2 * ((lane8 // 16) % 4) + (lane8 // 128) % 2) + 1
    near = [reach == kh for kh in range(3)]
    matrix = jnp.zeros((64, 8, 512), F32)
    for kh in range(3):
        piece = rows[kh * 64 : (kh + 1) * 64].reshape(64, 1, 512)
        matrix = jnp.where(near[kh][None], piece, matrix)
    w1[...] = matrix.reshape(512, 512).T.astype(BF)

    tile4 = (iota((32, 128), 0) == iota((32, 128), 1) % 32).astype(F32).astype(BF)
    wide = dot(f2b[...], tile4)
    group4 = iota((16, 128), 1) // 32
    parts = []
    for kd in range(3):
        for kw in range(3):
            for hq in range(4):
                block = jnp.zeros((16, 128), F32)
                for kh in range(3):
                    if 0 <= hq - kh + 1 < 4:
                        tap = (kd * 3 + kh) * 3 + kw
                        block = jnp.where(group4 == hq - kh + 1, wide[tap * 16 : tap * 16 + 16], block)
                parts.append(block)
    joined = jnp.concatenate(parts, axis=0)
    w2t[...] = joined.astype(BF)
    w2[...] = joined.T.astype(BF)

    bias_one = column(b1b[...], 16)
    bias_two = column(b2b[...], 32)
    take = iota((256, 512), 1)
    sample = (iota((256, 512), 0) == 2 * (take % 128) - 1 + take // 128).astype(F32).astype(BF)

    def split_columns(part):
        source = raw[:, part * RIM : part * RIM + 64, :].reshape(256, 256)
        columns = dot(source, sample).reshape(4, 64, 512)[:, 8:56]
        for s in range(4):
            shifted[s * 4 : s * 4 + 4, part * RIM : part * RIM + RIM] = columns[
                :, :, s * 128 : (s + 1) * 128
            ].astype(BF)

    lane64 = iota((64, 128), 1)

    def window(p):
        return shifted[:, p * 16 : p * 16 + 32, :].reshape(512, LANES)

    def layer_one(pair):
        both = dot(w1[...], jnp.concatenate([window(p) for p in pair], axis=1))
        for n, p in enumerate(pair):
            linear = both[:, n * 128 : (n + 1) * 128].reshape(32, 16, LANES) + bias_one[None]
            linear = linear.reshape(8, 64, LANES)
            slope = jnp.where(linear > 0, 1.0, 0.3)
            if 2 <= p <= 5:
                slopes[p - 2] = slope
            mean = jnp.sum(linear * slope, axis=0) * 0.125
            if p < 2:
                mean = jnp.where(first, 0.0, mean)
            if p > 5:
                mean = jnp.where(last, 0.0, mean)
            base = p * 192
            pooled[base : base + 64, :] = jnp.where(
                lane64 == 0, 0.0, pltpu.roll(mean, 1, axis=1)
            ).astype(BF)
            pooled[base + 64 : base + 128, :] = mean.astype(BF)
            pooled[base + 128 : base + 192, :] = jnp.where(
                lane64 == 127, 0.0, pltpu.roll(mean, 127, axis=1)
            ).astype(BF)

    def layer_two(pair):
        both = dot(
            w2[...],
            jnp.concatenate([pooled[j * 192 : j * 192 + 576, :] for j in pair], axis=1),
        )
        for n, j in enumerate(pair):
            linear = both[:, n * 128 : (n + 1) * 128].reshape(4, 32, LANES)
            linear = (linear + bias_two[None]).reshape(128, LANES)
            slope = jnp.where(linear > 0, 1.0, 0.3)
            errors_two[j * 128 : (j + 1) * 128, :] = (
                cots[j * 128 : (j + 1) * 128, :].astype(F32) * slope
            ).astype(BF)
            if 1 <= j <= 4:
                out = linear * slope
                for hq in range(4):
                    cotf[pl.ds((j - 1) * 4 + hq, 32, stride=16), :] = out[hq * 32 : (hq + 1) * 32]

    split_columns(1)
    layer_one((3, 4))

    @pl.when(jnp.logical_not(first))
    def _():
        halo(0).wait_recv()

    split_columns(0)

    @pl.when(jnp.logical_not(last))
    def _():
        halo(1).wait_recv()

    split_columns(2)
    layer_one((2, 5))
    layer_one((1, 6))
    layer_one((0, 7))
    layer_two((2, 3))
    layer_two((1, 4))

    @pl.when(jnp.logical_not(first))
    def _():
        halo(2).wait_recv()

    @pl.when(jnp.logical_not(last))
    def _():
        halo(3).wait_recv()

    layer_two((0, 5))
    act_here[...] = cotf[...].astype(BF).reshape(32, 16, LANES)
    act_store = pltpu.make_async_copy(act_here, act_out, out_sem.at[0])
    act_store.start()

    own = jnp.concatenate(
        [errors_two[j * 128 : (j + 1) * 128, :] for j in range(1, 5)], axis=1
    )
    near_in = jnp.concatenate(
        [pooled[j * 192 : j * 192 + 576, :] for j in range(1, 5)], axis=1
    )
    near_in = jnp.concatenate([near_in, jnp.ones((16, 512), BF)], axis=0)
    outer = dot_nt(near_in, own)
    taps = []
    for kd in range(3):
        for kh in range(3):
            for kw in range(3):
                block = jnp.zeros((16, 128), F32)
                for hq in range(4):
                    if 0 <= hq - kh + 1 < 4:
                        at = ((kd * 3 + kw) * 4 + hq) * 16
                        block = jnp.where(group4 == hq - kh + 1, outer[at : at + 16], block)
                taps.append(fold(block, (64, 32)))
    taps.append(fold(outer[576:592], (64, 32)))
    for q in range(7):
        block = taps[4 * q]
        for slot in range(1, 4):
            block = jnp.where(group4 == slot, taps[4 * q + slot], block)
        terms[2 * q] = block[0:8]
        terms[2 * q + 1] = block[8:16]

    terms[14] = jnp.zeros((8, 128), F32)
    terms[15] = jnp.zeros((8, 128), F32)

    share = TILES // space_n

    def scatter(k):
        to = lax.rem(me + k, space_n)
        return pltpu.make_async_remote_copy(
            src_ref=terms.at[pl.ds(to * share, share)],
            dst_ref=landed.at[k - 1],
            send_sem=rs_send.at[k - 1],
            recv_sem=rs_recv.at[k - 1],
            device_id={"space": to},
            device_id_type=MESH,
        )

    def swap(axis, count, k, source, buffer, send, recv):
        return pltpu.make_async_remote_copy(
            src_ref=buffer.at[source],
            dst_ref=buffer.at[source],
            send_sem=send.at[k - 1],
            recv_sem=recv.at[k - 1],
            device_id={axis: lax.rem(lax.axis_index(axis) + k, count)},
            device_id_type=MESH,
        )

    def swap_start(axis, count, *where):
        for k in range(1, count):
            swap(axis, count, k, lax.axis_index(axis), *where).start()

    def swap_sent(axis, count, *where):
        for k in range(1, count):
            swap(axis, count, k, lax.axis_index(axis), *where).wait_send()

    def swap_landed(axis, count, *where):
        for k in range(1, count):
            source = lax.rem(lax.axis_index(axis) + count - k, count)
            swap(axis, count, k, source, *where).wait_recv()

    early_dp = ("dp", dp_n, across, dp_send, dp_recv)
    early_all = ("space", space_n, total, ag_send, ag_recv)
    last_space = ("space", space_n, late_space, ls_send, ls_recv)
    last_dp = ("dp", dp_n, late_dp, ld_send, ld_recv)

    for k in range(1, space_n):
        scatter(k).start()

    back = jnp.concatenate([w2t[kd * 192 : (kd + 1) * 192, :] for kd in (2, 1, 0)], axis=1)
    quad = dot(
        back,
        jnp.concatenate([errors_two[q * 128 : q * 128 + 384, :] for q in range(4)], axis=1),
    )
    for q in range(4):
        three = quad[:, q * 128 : (q + 1) * 128]
        grad = three[64:128]
        grad = grad + jnp.where(lane64 == 127, 0.0, pltpu.roll(three[0:64], 127, axis=1))
        grad = grad + jnp.where(lane64 == 0, 0.0, pltpu.roll(three[128:192], 1, axis=1))
        grad = grad.astype(BF).astype(F32)
        for hq in range(4):
            pgf[pl.ds(q * 4 + hq, 16, stride=16), :] = grad[hq * 16 : (hq + 1) * 16]
        errors_one[:, q * 128 : (q + 1) * 128] = (
            ((grad * 0.125)[None] * slopes[q]).astype(BF).reshape(512, LANES)
        )
    pg_here[...] = pgf[...].astype(BF).reshape(16, 16, LANES)
    pg_store = pltpu.make_async_copy(pg_here, pg_out, out_sem.at[1])
    pg_store.start()

    sums = terms[pl.ds(me * share, share)]
    for k in range(1, space_n):
        scatter(k).wait_recv()
        sums = sums + landed[k - 1]
    across[mine] = sums
    swap_start(*early_dp)

    near_in = jnp.concatenate([window(p) for p in range(2, 6)], axis=1)
    near_in = jnp.concatenate([near_in, jnp.ones((16, 512), BF)], axis=0)
    outer = dot_nt(near_in, errors_one[...])
    body = outer[0:512].reshape(4, 4, 4, 8, 512)
    low = iota((4, 3, 8, 128), 3) < 64
    for kh in range(3):
        summed = jnp.zeros((4, 4, 3, 8, 128), F32)
        for part in range(4):
            dd = part // 2
            cut = body[:, :, dd : dd + 3, :, part * 128 : (part + 1) * 128]
            mask = near[kh][:, part * 128 : (part + 1) * 128]
            summed = summed + jnp.where(mask[None, None, None], cut, 0.0)
        for kw in range(3):
            both = jnp.where(low, summed[kw], summed[kw + 1])
            for kd in range(3):
                tap = (kd * 3 + kh) * 3 + kw
                stack[tap * 32 : tap * 32 + 32, :] = both[:, kd].reshape(32, LANES)
    ones = outer[512:520]
    ones = ones[:, 0:128] + ones[:, 128:256] + ones[:, 256:384] + ones[:, 384:512]
    stack[864:872, :] = jnp.where(iota((8, 128), 0) == 0, ones, 0.0)
    stack[872:896, :] = jnp.zeros((24, 128), F32)
    gather = (iota((112, 896), 0) == iota((112, 896), 1) // 8).astype(F32).astype(BF)
    whole = stack[...]
    high = whole.astype(BF)
    rest = (whole - high.astype(F32)).astype(BF)
    reduced = fold(dot(gather, high) + dot(gather, rest), (64, 32, 16))
    group8 = iota((8, 128), 1) // 16
    for half in range(2):
        block = jnp.zeros((8, 128), F32)
        for slot in range(8):
            v = half * 8 + slot
            if v < 14:
                block = jnp.where(group8 == slot, reduced[v * 8 : v * 8 + 8], block)
        late[half] = block

    late_space[me] = late[...]
    swap_start(*last_space)

    swap_landed(*early_dp)
    sums = across[0]
    for k in range(1, dp_n):
        sums = sums + across[k]
    total[me] = sums
    swap_start(*early_all)

    swap_landed(*last_space)
    sums = late_space[0]
    for k in range(1, space_n):
        sums = sums + late_space[k]
    late_dp[mine] = sums
    swap_start(*last_dp)

    swap_landed(*early_all)
    sums_here[0:TILES] = total[...].reshape(TILES, 8, 128)
    swap_landed(*last_dp)
    sums = late_dp[0]
    for k in range(1, dp_n):
        sums = sums + late_dp[k]
    sums_here[TILES : TILES + 2] = sums
    sums_store = pltpu.make_async_copy(sums_here, sums_out, out_sem.at[2])
    sums_store.start()

    for k in range(1, space_n):
        scatter(k).wait_send()
    swap_sent(*early_dp)
    swap_sent(*early_all)
    swap_sent(*last_space)
    swap_sent(*last_dp)
    act_store.wait()
    pg_store.wait()
    sums_store.wait()

    @pl.when(jnp.logical_not(last))
    def _():
        halo(0).wait_send()
        halo(2).wait_send()

    @pl.when(jnp.logical_not(first))
    def _():
        halo(1).wait_send()
        halo(3).wait_send()


def finish(scale_one, scale_two, act, pg, sums_in, act_out, pg_out, g1_out, s1_out, g2_out, s2_out,
           sums_here, g1, s1, g2, s2, sem):
    load = pltpu.make_async_copy(sums_in, sums_here, sem.at[6])
    load.start()
    big = [
        pltpu.make_async_copy(act, act_out, sem.at[0]),
        pltpu.make_async_copy(pg, pg_out, sem.at[1]),
    ]
    for copy in big:
        copy.start()
    load.wait()
    sums = sums_here[...]
    for q in range(7):
        block = jnp.concatenate([sums[2 * q], sums[2 * q + 1]], axis=0) * scale_two
        for slot in range(4):
            tap = 4 * q + slot
            turned = block if slot == 0 else pltpu.roll(block, 128 - 32 * slot, axis=1)
            if tap < 27:
                g2[tap * 16 : tap * 16 + 16, :] = turned[:, 0:32]
            else:
                s2[...] = turned[0:1, 0:32]
    for v in range(14):
        block = sums[TILES + v // 8] * scale_one
        slot = v % 8
        turned = block if slot == 0 else pltpu.roll(block, 128 - 16 * slot, axis=1)
        g1[2 * v] = turned[0:4, 0:16]
        if v < 13:
            g1[2 * v + 1] = turned[4:8, 0:16]
        else:
            s1[...] = turned[4:5, 0:16]
    small = [
        pltpu.make_async_copy(src, dst, sem.at[2 + n])
        for n, (src, dst) in enumerate(((g1, g1_out), (s1, s1_out), (g2, g2_out), (s2, s2_out)))
    ]
    for copy in small:
        copy.start()
    for copy in big + small:
        copy.wait()


def shards(dp_n, space_n, volume, first_filters, first_biases, second_filters, second_biases, cotangent):
    _, c_in, planes, high, wide = volume.shape
    c1, c2 = first_filters.shape[0], second_filters.shape[0]
    assert (c_in, planes, high, wide, c1, c2) == (4, 8, 8, 256, 16, 32)
    assert TILES % space_n == 0
    count_one = dp_n * space_n * planes * high * wide
    scale_one = 1.0 / math.sqrt(count_one)
    scale_two = 1.0 / math.sqrt(count_one / 8)
    share = TILES // space_n
    f1 = first_filters.transpose(2, 3, 4, 1, 0).reshape(27, 4, 16)
    f2 = second_filters.transpose(2, 3, 4, 1, 0).reshape(432, 32)
    vmem = pl.BlockSpec(memory_space=pltpu.VMEM)
    hbm = pl.BlockSpec(memory_space=pltpu.HBM)
    dma = pltpu.SemaphoreType.DMA
    act, pg, sums = pl.pallas_call(
        functools.partial(kernel, dp_n, space_n),
        out_shape=(
            jax.ShapeDtypeStruct((32, 16, 128), BF),
            jax.ShapeDtypeStruct((16, 16, 128), BF),
            jax.ShapeDtypeStruct((TILES + 2, 8, 128), F32),
        ),
        in_specs=[hbm] * 7,
        out_specs=(hbm,) * 3,
        scratch_shapes=[
            pltpu.VMEM((4, 2 * RIM + 64, 256), BF),
            pltpu.VMEM((32, 16, 128), BF),
            pltpu.VMEM((27, 4, 16), BF),
            pltpu.VMEM((128, 16), F32),
            pltpu.VMEM((432, 32), BF),
            pltpu.VMEM((1, 16), F32),
            pltpu.VMEM((1, 32), F32),
            pltpu.VMEM((768, 128), BF),
            pltpu.VMEM((768, 128), BF),
            pltpu.VMEM((512, 128), F32),
            pltpu.VMEM((16, 144, 128), BF),
            pltpu.VMEM((8 * 192, 128), BF),
            pltpu.VMEM((4, 8, 64, 128), F32),
            pltpu.VMEM((768, 128), BF),
            pltpu.VMEM((512, 512), BF),
            pltpu.VMEM((256, 128), F32),
            pltpu.VMEM((512, 512), BF),
            pltpu.VMEM((128, 576), BF),
            pltpu.VMEM((576, 128), BF),
            pltpu.VMEM((896, 128), F32),
            pltpu.VMEM((TILES, 8, 128), F32),
            pltpu.VMEM((space_n - 1, share, 8, 128), F32),
            pltpu.VMEM((dp_n, share, 8, 128), F32),
            pltpu.VMEM((space_n, share, 8, 128), F32),
            pltpu.VMEM((2, 8, 128), F32),
            pltpu.VMEM((space_n, 2, 8, 128), F32),
            pltpu.VMEM((dp_n, 2, 8, 128), F32),
            pltpu.VMEM((32, 16, 128), BF),
            pltpu.VMEM((16, 16, 128), BF),
            pltpu.VMEM((TILES + 2, 8, 128), F32),
            dma((3,)),
            dma((7,)),
            dma((4,)),
            dma((4,)),
        ]
        + [dma((space_n - 1,))] * 2
        + [dma((dp_n - 1,))] * 2
        + [dma((space_n - 1,))] * 4
        + [dma((dp_n - 1,))] * 2,
        compiler_params=pltpu.CompilerParams(
            collective_id=0, has_side_effects=True, vmem_limit_bytes=VMEM_LIMIT
        ),
    )(
        volume.reshape(4, 64, 256),
        cotangent.reshape(32, 16, 128),
        f1,
        f2,
        first_biases.reshape(1, 16),
        second_biases.reshape(1, 32),
        jnp.asarray(tap_choice(), BF),
    )
    act, pg, g1, s1, g2, s2 = pl.pallas_call(
        functools.partial(finish, scale_one, scale_two),
        out_shape=(
            jax.ShapeDtypeStruct((32, 16, 128), BF),
            jax.ShapeDtypeStruct((16, 16, 128), BF),
            jax.ShapeDtypeStruct((27, 4, 16), F32),
            jax.ShapeDtypeStruct((1, 16), F32),
            jax.ShapeDtypeStruct((432, 32), F32),
            jax.ShapeDtypeStruct((1, 32), F32),
        ),
        in_specs=[hbm] * 3,
        out_specs=(hbm,) * 6,
        scratch_shapes=[
            pltpu.VMEM((TILES + 2, 8, 128), F32),
            pltpu.VMEM((27, 4, 16), F32),
            pltpu.VMEM((1, 16), F32),
            pltpu.VMEM((432, 32), F32),
            pltpu.VMEM((1, 32), F32),
            dma((7,)),
        ],
        compiler_params=pltpu.CompilerParams(vmem_limit_bytes=VMEM_LIMIT),
    )(act, pg, sums)
    return (
        act.reshape(1, 32, 4, 4, 128),
        pg.reshape(1, 16, 4, 4, 128),
        g1.reshape(3, 3, 3, 4, 16).transpose(4, 3, 0, 1, 2),
        s1.reshape(16),
        g2.reshape(3, 3, 3, 16, 32).transpose(4, 3, 0, 1, 2),
        s2.reshape(32),
    )


def solution(mesh):
    placed = (
        P("dp", None, "space", None, None),
        P(),
        P(),
        P(),
        P(),
        P("dp", None, "space", None, None),
    )
    return jax.shard_map(
        functools.partial(shards, mesh.shape["dp"], mesh.shape["space"]),
        mesh=mesh,
        in_specs=placed,
        out_specs=(
            P("dp", None, "space", None, None),
            P("dp", None, "space", None, None),
            P(),
            P(),
            P(),
            P(),
        ),
        check_vma=False,
    )
```

time: 38 us -> 36.1 us (0.950)
  local copies, waits for them, and re-layouts: 7.83 us -> 0 us
  Pallas kernels: 29.3 us -> 35.3 us
    unnamed x17 -> x0, local copies, waits for them, and re-layouts: 6.38 us -> none
    pallas_call x1 -> x2, Pallas kernels: 29.3 us -> 35.3 us  [the longest x1 28.2 us: shards(): pl.pallas_call(functools.partial(kernel, dp_n, space_n), out_shape=(jax.S...]
    reshape x2 -> x0, local copies, waits for them, and re-layouts: 1.44 us -> none  [the longest x1 0.8 us: shards(): f1 = first_filters.transpose(2, 3, 4, 1, 0).reshape(108, 16)]
where the time goes in v2:
time: 36.1 us; the launch traced here: 36 us
  Pallas kernels  35.3 us (98%)
  between operations  0.64 us (2%)
    pallas_call x1, Pallas kernels, shards(): pl.pallas_call(functools.partial(kernel, dp_n, space_n), out_shape=(jax.S...  28.2 us
    pallas_call x1, Pallas kernels, shards(): pl.pallas_call(functools.partial(finish, scale_one, scale_two), out_shape...  7.13 us

profile of v2, /device:TPU:0, one launch (start us, length us, event | category | flops | bytes accessed | tf_op | source)
XLA Modules:
  0.0 36.0 jit_solution(9859507621745016189)
XLA Ops:
  0.6 28.2 %shard_map.118 = (bf16[32,16,128]{2,1,0:T(8,128)(2,1)}, bf16[16,16,128]{2,1,0:T(8,128)(2,1)}, f32[18,8,128]{2,1,0:T(8,128)}) custom-call(bf16[4,64,256]{2,1,0:T(8,128)(2,1)} %bitcast.20, bf16[32,16,128]{2,1,0:T(8,128)(2,1)} %bitcast.21, bf16[27,4,16]{2,1,0:T(4,128)(2,1)} %bitcast.23, bf16[432,32]{1,0:T(8,128)(2,1)} %bitcast.22, f32[1,16]{1,0:T(1,128)} %bitcast.24, ...), custom_call_target="tpu_custom_call" | custom-call | tf_op jit(solution)/shard_map/pallas_call | solution.py:524
  28.8 7.1 %shard_map.119 = (bf16[32,16,128]{2,1,0:T(8,128)(2,1)}, bf16[16,16,128]{2,1,0:T(8,128)(2,1)}, f32[27,4,16]{2,1,0:T(4,128)}, f32[1,16]{1,0:T(1,128)}, f32[432,32]{1,0:T(8,128)}, /*index=5*/f32[1,32]{1,0:T(1,128)}) custom-call(bf16[32,16,128]{2,1,0:T(8,128)(2,1)} %get-tuple-element.15.act, bf16[16,16,128]{2,1,0:T(8,128)(2,1)} %get-tuple-element.16.pg, ...), custom_call_target="tpu_custom_call" | custom-call | tf_op jit(solution)/shard_map/pallas_call | solution.py:585

commit v3 on v2

--- a/solution.py
+++ b/solution.py
@@ -354,9 +354,6 @@
     last_space = ("space", space_n, late_space, ls_send, ls_recv)
     last_dp = ("dp", dp_n, late_dp, ld_send, ld_recv)
 
-    for k in range(1, space_n):
-        scatter(k).start()
-
     back = jnp.concatenate([w2t[kd * 192 : (kd + 1) * 192, :] for kd in (2, 1, 0)], axis=1)
     quad = dot(
         back,
@@ -377,12 +374,8 @@
     pg_store = pltpu.make_async_copy(pg_here, pg_out, out_sem.at[1])
     pg_store.start()
 
-    sums = terms[pl.ds(me * share, share)]
     for k in range(1, space_n):
-        scatter(k).wait_recv()
-        sums = sums + landed[k - 1]
-    across[mine] = sums
-    swap_start(*early_dp)
+        scatter(k).start()
 
     near_in = jnp.concatenate([window(p) for p in range(2, 6)], axis=1)
     near_in = jnp.concatenate([near_in, jnp.ones((16, 512), BF)], axis=0)
@@ -422,19 +415,26 @@
     late_space[me] = late[...]
     swap_start(*last_space)
 
+    sums = terms[pl.ds(me * share, share)]
+    for k in range(1, space_n):
+        scatter(k).wait_recv()
+        sums = sums + landed[k - 1]
+    across[mine] = sums
+    swap_start(*early_dp)
+
+    swap_landed(*last_space)
+    sums = late_space[0]
+    for k in range(1, space_n):
+        sums = sums + late_space[k]
+    late_dp[mine] = sums
+    swap_start(*last_dp)
+
     swap_landed(*early_dp)
     sums = across[0]
     for k in range(1, dp_n):
         sums = sums + across[k]
     total[me] = sums
     swap_start(*early_all)
-
-    swap_landed(*last_space)
-    sums = late_space[0]
-    for k in range(1, space_n):
-        sums = sums + late_space[k]
-    late_dp[mine] = sums
-    swap_start(*last_dp)
 
     swap_landed(*early_all)
     sums_here[0:TILES] = total[...].reshape(TILES, 8, 128)
@@ -468,14 +468,21 @@
 
 
 def finish(scale_one, scale_two, act, pg, sums_in, act_out, pg_out, g1_out, s1_out, g2_out, s2_out,
-           sums_here, g1, s1, g2, s2, sem):
+           act_here, pg_here, sums_here, g1, s1, g2, s2, sem):
     load = pltpu.make_async_copy(sums_in, sums_here, sem.at[6])
     load.start()
+    loads = [
+        pltpu.make_async_copy(act, act_here, sem.at[7]),
+        pltpu.make_async_copy(pg, pg_here, sem.at[8]),
+    ]
+    for copy in loads:
+        copy.start()
     big = [
-        pltpu.make_async_copy(act, act_out, sem.at[0]),
-        pltpu.make_async_copy(pg, pg_out, sem.at[1]),
+        pltpu.make_async_copy(act_here, act_out, sem.at[0]),
+        pltpu.make_async_copy(pg_here, pg_out, sem.at[1]),
     ]
-    for copy in big:
+    for ready, copy in zip(loads, big):
+        ready.wait()
         copy.start()
     load.wait()
     sums = sums_here[...]
@@ -595,12 +602,14 @@
         in_specs=[hbm] * 3,
         out_specs=(hbm,) * 6,
         scratch_shapes=[
+            pltpu.VMEM((32, 16, 128), BF),
+            pltpu.VMEM((16, 16, 128), BF),
             pltpu.VMEM((TILES + 2, 8, 128), F32),
             pltpu.VMEM((27, 4, 16), F32),
             pltpu.VMEM((1, 16), F32),
             pltpu.VMEM((432, 32), F32),
             pltpu.VMEM((1, 32), F32),
-            dma((7,)),
+            dma((9,)),
         ],
         compiler_params=pltpu.CompilerParams(vmem_limit_bytes=VMEM_LIMIT),
     )(act, pg, sums)

time: 36.1 us -> 30.3 us (0.84)
  Pallas kernels: 35.3 us -> 29.5 us
    pallas_call x1, Pallas kernels: 7.13 us -> 1.83 us  [shards(): pl.pallas_call(functools.partial(finish, scale_one, scale_two), out_shape...]
    pallas_call x1, Pallas kernels: 28.2 us -> 27.6 us  [shards(): pl.pallas_call(functools.partial(kernel, dp_n, space_n), out_shape=(jax.S...]
where the time goes in v3:
time: 30.3 us; the launch traced here: 30.1 us
  Pallas kernels  29.5 us (97%)
  between operations  0.64 us (2%)
    pallas_call x1, Pallas kernels, shards(): pl.pallas_call(functools.partial(kernel, dp_n, space_n), out_shape=(jax.S...  27.6 us
    pallas_call x1, Pallas kernels, shards(): pl.pallas_call(functools.partial(finish, scale_one, scale_two), out_shape...  1.83 us

profile of v3, /device:TPU:0, one launch (start us, length us, event | category | flops | bytes accessed | tf_op | source)
XLA Modules:
  0.0 30.1 jit_solution(1963397724870972212)
XLA Ops:
  0.6 27.6 %shard_map.118 = (bf16[32,16,128]{2,1,0:T(8,128)(2,1)}, bf16[16,16,128]{2,1,0:T(8,128)(2,1)}, f32[18,8,128]{2,1,0:T(8,128)}) custom-call(bf16[4,64,256]{2,1,0:T(8,128)(2,1)} %bitcast.20, bf16[32,16,128]{2,1,0:T(8,128)(2,1)} %bitcast.21, bf16[27,4,16]{2,1,0:T(4,128)(2,1)} %bitcast.23, bf16[432,32]{1,0:T(8,128)(2,1)} %bitcast.22, f32[1,16]{1,0:T(1,128)} %bitcast.24, ...), custom_call_target="tpu_custom_call" | custom-call | tf_op jit(solution)/shard_map/pallas_call | solution.py:531
  28.3 1.8 %shard_map.119 = (bf16[32,16,128]{2,1,0:T(8,128)(2,1)}, bf16[16,16,128]{2,1,0:T(8,128)(2,1)}, f32[27,4,16]{2,1,0:T(4,128)}, f32[1,16]{1,0:T(1,128)}, f32[432,32]{1,0:T(8,128)}, /*index=5*/f32[1,32]{1,0:T(1,128)}) custom-call(bf16[32,16,128]{2,1,0:T(8,128)(2,1)} %get-tuple-element.15.act, bf16[16,16,128]{2,1,0:T(8,128)(2,1)} %get-tuple-element.16.pg, ...), custom_call_target="tpu_custom_call" | custom-call | tf_op jit(solution)/shard_map/pallas_call | solution.py:592

commit v4 on v3

--- a/solution.py
+++ b/solution.py
@@ -13,7 +13,7 @@
 F32 = jnp.float32
 MESH = pl.DeviceIdType.MESH
 LANES = 128
-RIM = 48
+RIM = 32
 VMEM_LIMIT = 60 * 1024 * 1024
 TILES = 16
 
@@ -102,22 +102,22 @@
     @pl.when(first)
     def _():
         raw[:, 0:RIM, :] = jnp.zeros((4, RIM, 256), BF)
-        cots[0:128, :] = jnp.zeros((128, LANES), BF)
+        errors_two[0:128, :] = jnp.zeros((128, LANES), BF)
 
     @pl.when(last)
     def _():
         raw[:, RIM + 64 :, :] = jnp.zeros((4, RIM, 256), BF)
-        cots[640:768, :] = jnp.zeros((128, LANES), BF)
+        errors_two[640:768, :] = jnp.zeros((128, LANES), BF)
 
     right = lax.rem(me + 1, space_n)
     left = lax.rem(me + space_n - 1, space_n)
 
     def halo(which):
         src, dst, to = (
-            (vol.at[:, 16:64], raw.at[:, 0:RIM], right),
+            (vol.at[:, 64 - RIM : 64], raw.at[:, 0:RIM], right),
             (vol.at[:, 0:RIM], raw.at[:, RIM + 64 : 2 * RIM + 64], left),
-            (cots.at[512:640], cots.at[0:128], right),
-            (cots.at[128:256], cots.at[640:768], left),
+            (errors_two.at[512:640], errors_two.at[0:128], right),
+            (errors_two.at[128:256], errors_two.at[640:768], left),
         )[which]
         return pltpu.make_async_remote_copy(
             src_ref=src,
@@ -142,17 +142,9 @@
     cotf[...] = cotb[...].reshape(512, LANES).astype(F32)
     for d in range(4):
         for hq in range(4):
-            cots[pl.ds((1 + d) * 128 + hq * 32, 32), :] = cotf[
+            cots[pl.ds(d * 128 + hq * 32, 32), :] = cotf[
                 pl.ds(d * 4 + hq, 32, stride=16), :
             ].astype(BF)
-
-    @pl.when(jnp.logical_not(last))
-    def _():
-        halo(2).start()
-
-    @pl.when(jnp.logical_not(first))
-    def _():
-        halo(3).start()
 
     for load in loads[1:]:
         load.wait()
@@ -199,11 +191,11 @@
     take = iota((256, 512), 1)
     sample = (iota((256, 512), 0) == 2 * (take % 128) - 1 + take // 128).astype(F32).astype(BF)
 
-    def split_columns(part):
-        source = raw[:, part * RIM : part * RIM + 64, :].reshape(256, 256)
-        columns = dot(source, sample).reshape(4, 64, 512)[:, 8:56]
+    def split_columns(start, rows, to):
+        source = raw[:, start : start + rows, :].reshape(4 * rows, 256)
+        columns = dot(source, sample).reshape(4, rows, 512)[:, 8 : rows - 8]
         for s in range(4):
-            shifted[s * 4 : s * 4 + 4, part * RIM : part * RIM + RIM] = columns[
+            shifted[s * 4 : s * 4 + 4, to : to + rows - 16] = columns[
                 :, :, s * 128 : (s + 1) * 128
             ].astype(BF)
 
@@ -218,12 +210,12 @@
             linear = both[:, n * 128 : (n + 1) * 128].reshape(32, 16, LANES) + bias_one[None]
             linear = linear.reshape(8, 64, LANES)
             slope = jnp.where(linear > 0, 1.0, 0.3)
-            if 2 <= p <= 5:
-                slopes[p - 2] = slope
+            if 1 <= p <= 4:
+                slopes[p - 1] = slope
             mean = jnp.sum(linear * slope, axis=0) * 0.125
-            if p < 2:
+            if p == 0:
                 mean = jnp.where(first, 0.0, mean)
-            if p > 5:
+            if p == 5:
                 mean = jnp.where(last, 0.0, mean)
             base = p * 192
             pooled[base : base + 64, :] = jnp.where(
@@ -243,43 +235,40 @@
             linear = both[:, n * 128 : (n + 1) * 128].reshape(4, 32, LANES)
             linear = (linear + bias_two[None]).reshape(128, LANES)
             slope = jnp.where(linear > 0, 1.0, 0.3)
-            errors_two[j * 128 : (j + 1) * 128, :] = (
+            errors_two[(j + 1) * 128 : (j + 2) * 128, :] = (
                 cots[j * 128 : (j + 1) * 128, :].astype(F32) * slope
             ).astype(BF)
-            if 1 <= j <= 4:
-                out = linear * slope
-                for hq in range(4):
-                    cotf[pl.ds((j - 1) * 4 + hq, 32, stride=16), :] = out[hq * 32 : (hq + 1) * 32]
-
-    split_columns(1)
-    layer_one((3, 4))
+            out = linear * slope
+            for hq in range(4):
+                cotf[pl.ds(j * 4 + hq, 32, stride=16), :] = out[hq * 32 : (hq + 1) * 32]
+
+    split_columns(RIM, 64, 32)
+    layer_one((2, 3))
 
     @pl.when(jnp.logical_not(first))
     def _():
         halo(0).wait_recv()
 
-    split_columns(0)
+    split_columns(0, 48, 0)
 
     @pl.when(jnp.logical_not(last))
     def _():
         halo(1).wait_recv()
 
-    split_columns(2)
-    layer_one((2, 5))
-    layer_one((1, 6))
-    layer_one((0, 7))
-    layer_two((2, 3))
-    layer_two((1, 4))
+    split_columns(80, 48, 80)
+    layer_one((0, 5))
+    layer_one((1, 4))
+    layer_two((0, 3))
+
+    @pl.when(jnp.logical_not(last))
+    def _():
+        halo(2).start()
 
     @pl.when(jnp.logical_not(first))
     def _():
-        halo(2).wait_recv()
-
-    @pl.when(jnp.logical_not(last))
-    def _():
-        halo(3).wait_recv()
-
-    layer_two((0, 5))
+        halo(3).start()
+
+    layer_two((1, 2))
     act_here[...] = cotf[...].astype(BF).reshape(32, 16, LANES)
     act_store = pltpu.make_async_copy(act_here, act_out, out_sem.at[0])
     act_store.start()
@@ -288,7 +277,7 @@
         [errors_two[j * 128 : (j + 1) * 128, :] for j in range(1, 5)], axis=1
     )
     near_in = jnp.concatenate(
-        [pooled[j * 192 : j * 192 + 576, :] for j in range(1, 5)], axis=1
+        [pooled[j * 192 : j * 192 + 576, :] for j in range(4)], axis=1
     )
     near_in = jnp.concatenate([near_in, jnp.ones((16, 512), BF)], axis=0)
     outer = dot_nt(near_in, own)
@@ -355,21 +344,35 @@
     last_dp = ("dp", dp_n, late_dp, ld_send, ld_recv)
 
     back = jnp.concatenate([w2t[kd * 192 : (kd + 1) * 192, :] for kd in (2, 1, 0)], axis=1)
-    quad = dot(
-        back,
-        jnp.concatenate([errors_two[q * 128 : q * 128 + 384, :] for q in range(4)], axis=1),
-    )
-    for q in range(4):
-        three = quad[:, q * 128 : (q + 1) * 128]
-        grad = three[64:128]
-        grad = grad + jnp.where(lane64 == 127, 0.0, pltpu.roll(three[0:64], 127, axis=1))
-        grad = grad + jnp.where(lane64 == 0, 0.0, pltpu.roll(three[128:192], 1, axis=1))
-        grad = grad.astype(BF).astype(F32)
-        for hq in range(4):
-            pgf[pl.ds(q * 4 + hq, 16, stride=16), :] = grad[hq * 16 : (hq + 1) * 16]
-        errors_one[:, q * 128 : (q + 1) * 128] = (
-            ((grad * 0.125)[None] * slopes[q]).astype(BF).reshape(512, LANES)
-        )
+
+    def spread_back(pair):
+        both = dot(
+            back,
+            jnp.concatenate([errors_two[q * 128 : q * 128 + 384, :] for q in pair], axis=1),
+        )
+        for n, q in enumerate(pair):
+            three = both[:, n * 128 : (n + 1) * 128]
+            grad = three[64:128]
+            grad = grad + jnp.where(lane64 == 127, 0.0, pltpu.roll(three[0:64], 127, axis=1))
+            grad = grad + jnp.where(lane64 == 0, 0.0, pltpu.roll(three[128:192], 1, axis=1))
+            grad = grad.astype(BF).astype(F32)
+            for hq in range(4):
+                pgf[pl.ds(q * 4 + hq, 16, stride=16), :] = grad[hq * 16 : (hq + 1) * 16]
+            errors_one[:, q * 128 : (q + 1) * 128] = (
+                ((grad * 0.125)[None] * slopes[q]).astype(BF).reshape(512, LANES)
+            )
+
+    spread_back((1, 2))
+
+    @pl.when(jnp.logical_not(first))
+    def _():
+        halo(2).wait_recv()
+
+    @pl.when(jnp.logical_not(last))
+    def _():
+        halo(3).wait_recv()
+
+    spread_back((0, 3))
     pg_here[...] = pgf[...].astype(BF).reshape(16, 16, LANES)
     pg_store = pltpu.make_async_copy(pg_here, pg_out, out_sem.at[1])
     pg_store.start()
@@ -377,7 +380,7 @@
     for k in range(1, space_n):
         scatter(k).start()
 
-    near_in = jnp.concatenate([window(p) for p in range(2, 6)], axis=1)
+    near_in = jnp.concatenate([window(p) for p in range(1, 5)], axis=1)
     near_in = jnp.concatenate([near_in, jnp.ones((16, 512), BF)], axis=0)
     outer = dot_nt(near_in, errors_one[...])
     body = outer[0:512].reshape(4, 4, 4, 8, 512)
@@ -546,10 +549,10 @@
             pltpu.VMEM((1, 16), F32),
             pltpu.VMEM((1, 32), F32),
             pltpu.VMEM((768, 128), BF),
-            pltpu.VMEM((768, 128), BF),
+            pltpu.VMEM((512, 128), BF),
             pltpu.VMEM((512, 128), F32),
-            pltpu.VMEM((16, 144, 128), BF),
-            pltpu.VMEM((8 * 192, 128), BF),
+            pltpu.VMEM((16, 112, 128), BF),
+            pltpu.VMEM((6 * 192, 128), BF),
             pltpu.VMEM((4, 8, 64, 128), F32),
             pltpu.VMEM((768, 128), BF),
             pltpu.VMEM((512, 512), BF),

time: 30.3 us -> 30.8 us (1.017)
  Pallas kernels: 29.5 us -> 30 us
    pallas_call x1, Pallas kernels: 27.6 us -> 28.1 us  [shards(): pl.pallas_call(functools.partial(kernel, dp_n, space_n), out_shape=(jax.S...]
where the time goes in v4:
time: 30.8 us; the launch traced here: 30.6 us
  Pallas kernels  30 us (97%)
  between operations  0.64 us (2%)
    pallas_call x1, Pallas kernels, shards(): pl.pallas_call(functools.partial(kernel, dp_n, space_n), out_shape=(jax.S...  28.1 us
    pallas_call x1, Pallas kernels, shards(): pl.pallas_call(functools.partial(finish, scale_one, scale_two), out_shape...  1.83 us

profile of v4, /device:TPU:0, one launch (start us, length us, event | category | flops | bytes accessed | tf_op | source)
XLA Modules:
  0.0 30.6 jit_solution(13127207112081661778)
XLA Ops:
  0.6 28.1 %shard_map.118 = (bf16[32,16,128]{2,1,0:T(8,128)(2,1)}, bf16[16,16,128]{2,1,0:T(8,128)(2,1)}, f32[18,8,128]{2,1,0:T(8,128)}) custom-call(bf16[4,64,256]{2,1,0:T(8,128)(2,1)} %bitcast.20, bf16[32,16,128]{2,1,0:T(8,128)(2,1)} %bitcast.21, bf16[27,4,16]{2,1,0:T(4,128)(2,1)} %bitcast.23, bf16[432,32]{1,0:T(8,128)(2,1)} %bitcast.22, f32[1,16]{1,0:T(1,128)} %bitcast.24, ...), custom_call_target="tpu_custom_call" | custom-call | tf_op jit(solution)/shard_map/pallas_call | solution.py:534
  28.8 1.8 %shard_map.119 = (bf16[32,16,128]{2,1,0:T(8,128)(2,1)}, bf16[16,16,128]{2,1,0:T(8,128)(2,1)}, f32[27,4,16]{2,1,0:T(4,128)}, f32[1,16]{1,0:T(1,128)}, f32[432,32]{1,0:T(8,128)}, /*index=5*/f32[1,32]{1,0:T(1,128)}) custom-call(bf16[32,16,128]{2,1,0:T(8,128)(2,1)} %get-tuple-element.15.act, bf16[16,16,128]{2,1,0:T(8,128)(2,1)} %get-tuple-element.16.pg, ...), custom_call_target="tpu_custom_call" | custom-call | tf_op jit(solution)/shard_map/pallas_call | solution.py:595

commit v5 on v3

--- a/solution.py
+++ b/solution.py
@@ -156,27 +156,30 @@
 
     for load in loads[1:]:
         load.wait()
-    f1f[104:128, :] = jnp.zeros((24, 16), F32)
+    f1f[...] = jnp.zeros((128, 128), F32)
     for tap in range(27):
-        f1f[tap * 4 : tap * 4 + 4, :] = f1b[tap].astype(F32)
-
-    lane = iota((64, 512), 1)
-    group = iota((64, 512), 0)
-    spread = (
-        (lane % 16 == group % 16) & (lane // 256 == group // 32) & ((lane // 64) % 2 == (group // 16) % 2)
-    ).astype(F32).astype(BF)
-    picked = dot(chosen[...], f1f[...].astype(BF)).astype(BF)
-    rows = jnp.concatenate([picked[g * 192 : (g + 1) * 192] for g in range(4)], axis=1)
-    rows = dot(rows, spread)
+        f1f[tap * 4 : tap * 4 + 4, 0:16] = f1b[tap].astype(F32)
+
+    picked = dot_nt(f1f[...].T[0:16].astype(BF), chosen[...])
+    picked = jnp.concatenate([picked[:, g * 64 : (g + 1) * 64] for g in range(12)], axis=0)
+    repeat = (iota((64, 512), 0) == iota((64, 512), 1) // 8).astype(F32).astype(BF)
+    rows = dot(picked.astype(BF), repeat)
+    height = iota((16, 512), 1) % 8
+    for dd in range(2):
+        for hpar in range(2):
+            for wpar in range(2):
+                for hq in range(4):
+                    block = jnp.zeros((16, 512), F32)
+                    for kh in range(3):
+                        at = ((dd * 2 + wpar) * 3 + kh) * 16
+                        block = jnp.where(
+                            height == 2 * hq + hpar + kh - 1, rows[at : at + 16], block
+                        )
+                    at = (((dd * 2 + hpar) * 2 + wpar) * 4 + hq) * 16
+                    w1[at : at + 16, :] = block.astype(BF)
     lane8 = iota((8, 512), 1)
     reach = iota((8, 512), 0) - (2 * ((lane8 // 16) % 4) + (lane8 // 128) % 2) + 1
     near = [reach == kh for kh in range(3)]
-    matrix = jnp.zeros((64, 8, 512), F32)
-    for kh in range(3):
-        piece = rows[kh * 64 : (kh + 1) * 64].reshape(64, 1, 512)
-        matrix = jnp.where(near[kh][None], piece, matrix)
-    w1[...] = matrix.reshape(512, 512).T.astype(BF)
-
     tile4 = (iota((32, 128), 0) == iota((32, 128), 1) % 32).astype(F32).astype(BF)
     wide = dot(f2b[...], tile4)
     group4 = iota((16, 128), 1) // 32
@@ -354,6 +357,9 @@
     last_space = ("space", space_n, late_space, ls_send, ls_recv)
     last_dp = ("dp", dp_n, late_dp, ld_send, ld_recv)
 
+    for k in range(1, space_n):
+        scatter(k).start()
+
     back = jnp.concatenate([w2t[kd * 192 : (kd + 1) * 192, :] for kd in (2, 1, 0)], axis=1)
     quad = dot(
         back,
@@ -373,9 +379,6 @@
     pg_here[...] = pgf[...].astype(BF).reshape(16, 16, LANES)
     pg_store = pltpu.make_async_copy(pg_here, pg_out, out_sem.at[1])
     pg_store.start()
-
-    for k in range(1, space_n):
-        scatter(k).start()
 
     near_in = jnp.concatenate([window(p) for p in range(2, 6)], axis=1)
     near_in = jnp.concatenate([near_in, jnp.ones((16, 512), BF)], axis=0)
@@ -398,6 +401,13 @@
     ones = ones[:, 0:128] + ones[:, 128:256] + ones[:, 256:384] + ones[:, 384:512]
     stack[864:872, :] = jnp.where(iota((8, 128), 0) == 0, ones, 0.0)
     stack[872:896, :] = jnp.zeros((24, 128), F32)
+    sums = terms[pl.ds(me * share, share)]
+    for k in range(1, space_n):
+        scatter(k).wait_recv()
+        sums = sums + landed[k - 1]
+    across[mine] = sums
+    swap_start(*early_dp)
+
     gather = (iota((112, 896), 0) == iota((112, 896), 1) // 8).astype(F32).astype(BF)
     whole = stack[...]
     high = whole.astype(BF)
@@ -415,12 +425,12 @@
     late_space[me] = late[...]
     swap_start(*last_space)
 
-    sums = terms[pl.ds(me * share, share)]
-    for k in range(1, space_n):
-        scatter(k).wait_recv()
-        sums = sums + landed[k - 1]
-    across[mine] = sums
-    swap_start(*early_dp)
+    swap_landed(*early_dp)
+    sums = across[0]
+    for k in range(1, dp_n):
+        sums = sums + across[k]
+    total[me] = sums
+    swap_start(*early_all)
 
     swap_landed(*last_space)
     sums = late_space[0]
@@ -428,13 +438,6 @@
         sums = sums + late_space[k]
     late_dp[mine] = sums
     swap_start(*last_dp)
-
-    swap_landed(*early_dp)
-    sums = across[0]
-    for k in range(1, dp_n):
-        sums = sums + across[k]
-    total[me] = sums
-    swap_start(*early_all)
 
     swap_landed(*early_all)
     sums_here[0:TILES] = total[...].reshape(TILES, 8, 128)
@@ -541,7 +544,7 @@
             pltpu.VMEM((4, 2 * RIM + 64, 256), BF),
             pltpu.VMEM((32, 16, 128), BF),
             pltpu.VMEM((27, 4, 16), BF),
-            pltpu.VMEM((128, 16), F32),
+            pltpu.VMEM((128, 128), F32),
             pltpu.VMEM((432, 32), BF),
             pltpu.VMEM((1, 16), F32),
             pltpu.VMEM((1, 32), F32),

time: 30.3 us -> 30.3 us (level)
  no operation moved by 1% of the time
where the time goes in v5:
time: 30.3 us; the launch traced here: 30.1 us
  Pallas kernels  29.5 us (97%)
  between operations  0.64 us (2%)
    pallas_call x1, Pallas kernels, shards(): pl.pallas_call(functools.partial(kernel, dp_n, space_n), out_shape=(jax.S...  27.6 us
    pallas_call x1, Pallas kernels, shards(): pl.pallas_call(functools.partial(finish, scale_one, scale_two), out_shape...  1.83 us

profile of v5, /device:TPU:0, one launch (start us, length us, event | category | flops | bytes accessed | tf_op | source)
XLA Modules:
  0.0 30.1 jit_solution(15802409139365040148)
XLA Ops:
  0.6 27.6 %shard_map.118 = (bf16[32,16,128]{2,1,0:T(8,128)(2,1)}, bf16[16,16,128]{2,1,0:T(8,128)(2,1)}, f32[18,8,128]{2,1,0:T(8,128)}) custom-call(bf16[4,64,256]{2,1,0:T(8,128)(2,1)} %bitcast.20, bf16[32,16,128]{2,1,0:T(8,128)(2,1)} %bitcast.21, bf16[27,4,16]{2,1,0:T(4,128)(2,1)} %bitcast.23, bf16[432,32]{1,0:T(8,128)(2,1)} %bitcast.22, f32[1,16]{1,0:T(1,128)} %bitcast.24, ...), custom_call_target="tpu_custom_call" | custom-call | tf_op jit(solution)/shard_map/pallas_call | solution.py:534
  28.3 1.8 %shard_map.119 = (bf16[32,16,128]{2,1,0:T(8,128)(2,1)}, bf16[16,16,128]{2,1,0:T(8,128)(2,1)}, f32[27,4,16]{2,1,0:T(4,128)}, f32[1,16]{1,0:T(1,128)}, f32[432,32]{1,0:T(8,128)}, /*index=5*/f32[1,32]{1,0:T(1,128)}) custom-call(bf16[32,16,128]{2,1,0:T(8,128)(2,1)} %get-tuple-element.15.act, bf16[16,16,128]{2,1,0:T(8,128)(2,1)} %get-tuple-element.16.pg, ...), custom_call_target="tpu_custom_call" | custom-call | tf_op jit(solution)/shard_map/pallas_call | solution.py:595

commit v6 on v5

--- a/solution.py
+++ b/solution.py
@@ -422,8 +422,8 @@
                 block = jnp.where(group8 == slot, reduced[v * 8 : v * 8 + 8], block)
         late[half] = block
 
-    late_space[me] = late[...]
-    swap_start(*last_space)
+    late_dp[mine] = late[...]
+    swap_start(*last_dp)
 
     swap_landed(*early_dp)
     sums = across[0]
@@ -432,19 +432,19 @@
     total[me] = sums
     swap_start(*early_all)
 
+    swap_landed(*last_dp)
+    sums = late_dp[0]
+    for k in range(1, dp_n):
+        sums = sums + late_dp[k]
+    late_space[me] = sums
+    swap_start(*last_space)
+
+    swap_landed(*early_all)
+    sums_here[0:TILES] = total[...].reshape(TILES, 8, 128)
     swap_landed(*last_space)
     sums = late_space[0]
     for k in range(1, space_n):
         sums = sums + late_space[k]
-    late_dp[mine] = sums
-    swap_start(*last_dp)
-
-    swap_landed(*early_all)
-    sums_here[0:TILES] = total[...].reshape(TILES, 8, 128)
-    swap_landed(*last_dp)
-    sums = late_dp[0]
-    for k in range(1, dp_n):
-        sums = sums + late_dp[k]
     sums_here[TILES : TILES + 2] = sums
     sums_store = pltpu.make_async_copy(sums_here, sums_out, out_sem.at[2])
     sums_store.start()

time: 30.3 us -> 31.1 us (1.026)
  Pallas kernels: 29.5 us -> 30.3 us
    pallas_call x1, Pallas kernels: 27.6 us -> 28.5 us  [shards(): pl.pallas_call(functools.partial(kernel, dp_n, space_n), out_shape=(jax.S...]
where the time goes in v6:
time: 31.1 us; the launch traced here: 31 us
  Pallas kernels  30.3 us (97%)
  between operations  0.64 us (2%)
    pallas_call x1, Pallas kernels, shards(): pl.pallas_call(functools.partial(kernel, dp_n, space_n), out_shape=(jax.S...  28.5 us
    pallas_call x1, Pallas kernels, shards(): pl.pallas_call(functools.partial(finish, scale_one, scale_two), out_shape...  1.83 us

profile of v6, /device:TPU:0, one launch (start us, length us, event | category | flops | bytes accessed | tf_op | source)
XLA Modules:
  0.0 31.0 jit_solution(3463892660423023947)
XLA Ops:
  0.6 28.5 %shard_map.118 = (bf16[32,16,128]{2,1,0:T(8,128)(2,1)}, bf16[16,16,128]{2,1,0:T(8,128)(2,1)}, f32[18,8,128]{2,1,0:T(8,128)}) custom-call(bf16[4,64,256]{2,1,0:T(8,128)(2,1)} %bitcast.20, bf16[32,16,128]{2,1,0:T(8,128)(2,1)} %bitcast.21, bf16[27,4,16]{2,1,0:T(4,128)(2,1)} %bitcast.23, bf16[432,32]{1,0:T(8,128)(2,1)} %bitcast.22, f32[1,16]{1,0:T(1,128)} %bitcast.24, ...), custom_call_target="tpu_custom_call" | custom-call | tf_op jit(solution)/shard_map/pallas_call | solution.py:534
  29.1 1.8 %shard_map.119 = (bf16[32,16,128]{2,1,0:T(8,128)(2,1)}, bf16[16,16,128]{2,1,0:T(8,128)(2,1)}, f32[27,4,16]{2,1,0:T(4,128)}, f32[1,16]{1,0:T(1,128)}, f32[432,32]{1,0:T(8,128)}, /*index=5*/f32[1,32]{1,0:T(1,128)}) custom-call(bf16[32,16,128]{2,1,0:T(8,128)(2,1)} %get-tuple-element.15.act, bf16[16,16,128]{2,1,0:T(8,128)(2,1)} %get-tuple-element.16.pg, ...), custom_call_target="tpu_custom_call" | custom-call | tf_op jit(solution)/shard_map/pallas_call | solution.py:595

commit v7 on v5

--- a/solution.py
+++ b/solution.py
@@ -357,9 +357,6 @@
     last_space = ("space", space_n, late_space, ls_send, ls_recv)
     last_dp = ("dp", dp_n, late_dp, ld_send, ld_recv)
 
-    for k in range(1, space_n):
-        scatter(k).start()
-
     back = jnp.concatenate([w2t[kd * 192 : (kd + 1) * 192, :] for kd in (2, 1, 0)], axis=1)
     quad = dot(
         back,
@@ -379,6 +376,9 @@
     pg_here[...] = pgf[...].astype(BF).reshape(16, 16, LANES)
     pg_store = pltpu.make_async_copy(pg_here, pg_out, out_sem.at[1])
     pg_store.start()
+
+    for k in range(1, space_n):
+        scatter(k).start()
 
     near_in = jnp.concatenate([window(p) for p in range(2, 6)], axis=1)
     near_in = jnp.concatenate([near_in, jnp.ones((16, 512), BF)], axis=0)
@@ -401,13 +401,6 @@
     ones = ones[:, 0:128] + ones[:, 128:256] + ones[:, 256:384] + ones[:, 384:512]
     stack[864:872, :] = jnp.where(iota((8, 128), 0) == 0, ones, 0.0)
     stack[872:896, :] = jnp.zeros((24, 128), F32)
-    sums = terms[pl.ds(me * share, share)]
-    for k in range(1, space_n):
-        scatter(k).wait_recv()
-        sums = sums + landed[k - 1]
-    across[mine] = sums
-    swap_start(*early_dp)
-
     gather = (iota((112, 896), 0) == iota((112, 896), 1) // 8).astype(F32).astype(BF)
     whole = stack[...]
     high = whole.astype(BF)
@@ -425,19 +418,26 @@
     late_space[me] = late[...]
     swap_start(*last_space)
 
+    sums = terms[pl.ds(me * share, share)]
+    for k in range(1, space_n):
+        scatter(k).wait_recv()
+        sums = sums + landed[k - 1]
+    across[mine] = sums
+    swap_start(*early_dp)
+
+    swap_landed(*last_space)
+    sums = late_space[0]
+    for k in range(1, space_n):
+        sums = sums + late_space[k]
+    late_dp[mine] = sums
+    swap_start(*last_dp)
+
     swap_landed(*early_dp)
     sums = across[0]
     for k in range(1, dp_n):
         sums = sums + across[k]
     total[me] = sums
     swap_start(*early_all)
-
-    swap_landed(*last_space)
-    sums = late_space[0]
-    for k in range(1, space_n):
-        sums = sums + late_space[k]
-    late_dp[mine] = sums
-    swap_start(*last_dp)
 
     swap_landed(*early_all)
     sums_here[0:TILES] = total[...].reshape(TILES, 8, 128)

time: 30.3 us -> 30.3 us (level)
  no operation moved by 1% of the time
where the time goes in v7:
time: 30.3 us; the launch traced here: 30.1 us
  Pallas kernels  29.5 us (97%)
  between operations  0.64 us (2%)
    pallas_call x1, Pallas kernels, shards(): pl.pallas_call(functools.partial(kernel, dp_n, space_n), out_shape=(jax.S...  27.6 us
    pallas_call x1, Pallas kernels, shards(): pl.pallas_call(functools.partial(finish, scale_one, scale_two), out_shape...  1.83 us

profile of v7, /device:TPU:0, one launch (start us, length us, event | category | flops | bytes accessed | tf_op | source)
XLA Modules:
  0.0 30.1 jit_solution(2310905721058934625)
XLA Ops:
  0.6 27.6 %shard_map.118 = (bf16[32,16,128]{2,1,0:T(8,128)(2,1)}, bf16[16,16,128]{2,1,0:T(8,128)(2,1)}, f32[18,8,128]{2,1,0:T(8,128)}) custom-call(bf16[4,64,256]{2,1,0:T(8,128)(2,1)} %bitcast.20, bf16[32,16,128]{2,1,0:T(8,128)(2,1)} %bitcast.21, bf16[27,4,16]{2,1,0:T(4,128)(2,1)} %bitcast.23, bf16[432,32]{1,0:T(8,128)(2,1)} %bitcast.22, f32[1,16]{1,0:T(1,128)} %bitcast.24, ...), custom_call_target="tpu_custom_call" | custom-call | tf_op jit(solution)/shard_map/pallas_call | solution.py:534
  28.3 1.8 %shard_map.119 = (bf16[32,16,128]{2,1,0:T(8,128)(2,1)}, bf16[16,16,128]{2,1,0:T(8,128)(2,1)}, f32[27,4,16]{2,1,0:T(4,128)}, f32[1,16]{1,0:T(1,128)}, f32[432,32]{1,0:T(8,128)}, /*index=5*/f32[1,32]{1,0:T(1,128)}) custom-call(bf16[32,16,128]{2,1,0:T(8,128)(2,1)} %get-tuple-element.15.act, bf16[16,16,128]{2,1,0:T(8,128)(2,1)} %get-tuple-element.16.pg, ...), custom_call_target="tpu_custom_call" | custom-call | tf_op jit(solution)/shard_map/pallas_call | solution.py:595
